TPU v7x, 512 devices: a whole 4x8x8 slice. The times are simulated.
512 devices in a mesh: grp: 8 (over y), reply: 16 (over x, z_lo), head: 4 (over z_hi, core).
Axes of the slice: x: 4, y: 8, z: 8 (z_hi: 2, z_lo: 4; z = z_hi * 4 + z_lo), core: 2. Of those that a mesh axis runs over, the one named last changes fastest.
Arguments:
- queries: bfloat16 [8, 16, 256, 4096], P('grp', 'reply', None, 'head'), may hold values from -4.5 to 4.5
- reply_kv: bfloat16 [8, 16, 2, 256, 512], P('grp', 'reply', None, None, 'head'), may hold values from -6 to 6
- prompt_kv: bfloat16 [8, 2, 1024, 512], P('grp', None, 'reply', 'head'), may hold values from -4.5 to 4.5
- saved_out: bfloat16 [8, 16, 256, 4096], P('grp', 'reply', None, 'head'), may hold values from -6 to 6
- grad_out: bfloat16 [8, 16, 256, 4096], P('grp', 'reply', None, 'head'), may hold values from -6 to 6
- prompt_len: int32 [8], P('grp'), may hold values from 128 to 1024
- reply_len: int32 [8, 16], P('grp', 'reply'), may hold values from 1 to 256, as said below
Outputs:
- query_grad: bfloat16 [8, 16, 256, 4096], P('grp', 'reply', None, 'head')
- reply_kv_grad: bfloat16 [8, 16, 2, 256, 512], P('grp', 'reply', None, None, 'head')
- prompt_kv_grad: bfloat16 [8, 2, 1024, 512], P('grp', None, 'reply', 'head')
- value_bias_grad: float32 [512], P('head')
Inputs may be any that keep to these rules, and one draw needn't show every extreme that they name: `reply_len`: live tokens of each reply; every group has a reply of 256 tokens.
All inputs are finite; a program needn't handle non-finite values.
Results may differ from a plain program's by a relative error of at most 0.0049.
Values may be sent and summed in bfloat16 or wider, within the bound.
A program may use at most 64 MiB of HBM per device.

v0:
```python
import math

import jax
import jax.numpy as jnp
from jax import lax
from jax.sharding import PartitionSpec as P

NEGATIVE = -1e30
key_block_rows = 256


def on_device(queries, reply_kv, prompt_kv, saved_out, grad_out, prompt_len, reply_len):
    row_total = queries.shape[2]
    head_size = reply_kv.shape[-1]
    shared = queries.shape[3] // head_size
    factor = head_size ** (-0.5)
    query = queries[0, 0].reshape(row_total, shared, head_size)
    own_keys = reply_kv[0, 0, 0]
    own_values = reply_kv[0, 0, 1]
    prompt_limit = prompt_len[0]
    reply_limit = reply_len[0, 0]
    positions = jnp.arange(row_total, dtype=jnp.int32)
    out_grad = jnp.where(
        (positions < reply_limit)[:, None], grad_out[0, 0], jnp.zeros((), jnp.bfloat16)
    )
    out_grad = out_grad.reshape(row_total, shared, head_size)
    saved = saved_out[0, 0].reshape(row_total, shared, head_size)
    row_dots = jnp.einsum("tjd,tjd->jt", out_grad, saved, preferred_element_type=jnp.float32)
    causal = positions[None, :] <= positions[:, None]

    def scores(key_block, key_mask):
        raw = (
            jnp.einsum("tjd,kd->jtk", query, key_block, preferred_element_type=jnp.float32) * factor
        )
        return jnp.where(key_mask[None], raw, NEGATIVE)

    def add_stats(running, key_block, key_mask):
        highest, total = running
        logits = scores(key_block, key_mask)
        new_high = jnp.maximum(highest, jnp.max(logits, axis=-1))
        total = total * jnp.exp(highest - new_high) + jnp.sum(
            jnp.exp(logits - new_high[..., None]), axis=-1
        )
        return (new_high, total)

    def score_terms(key_block, value_block, key_mask, log_total):
        logits = scores(key_block, key_mask)
        prob = jnp.exp(logits - log_total[..., None])
        prob_grad = jnp.einsum(
            "tjd,kd->jtk", out_grad, value_block, preferred_element_type=jnp.float32
        )
        score_grad = (prob * (prob_grad - row_dots[..., None])).astype(jnp.bfloat16)
        return (prob, score_grad)

    def key_value_parts(prob, score_grad):
        prob_half = prob.astype(jnp.bfloat16)
        key_part = (
            jnp.einsum("jtk,tjd->kd", score_grad, query, preferred_element_type=jnp.float32)
            * factor
        )
        value_part = jnp.einsum(
            "jtk,tjd->kd", prob_half, out_grad, preferred_element_type=jnp.float32
        )
        return (key_part, value_part)

    def block_grads(key_block, value_block, key_mask, log_total):
        prob, score_grad = score_terms(key_block, value_block, key_mask, log_total)
        query_part = jnp.einsum(
            "jtk,kd->tjd", score_grad, key_block, preferred_element_type=jnp.float32
        )
        key_part, value_part = key_value_parts(prob, score_grad)
        return (query_part, key_part, value_part)

    running = (
        jnp.full((shared, row_total), NEGATIVE, jnp.float32),
        jnp.zeros((shared, row_total), jnp.float32),
    )
    running = add_stats(running, own_keys, causal)
    columns = prompt_kv[0]
    local_rows = columns.shape[1]
    prompt_rows = local_rows * lax.axis_size("reply")
    query_empty = jnp.zeros((row_total, shared, head_size), jnp.float32)
    empty = (query_empty, jnp.zeros((2, prompt_rows, head_size), jnp.float32))
    gathered = lax.all_gather(columns, "reply", axis=1, tiled=True)
    row_count = gathered.shape[1]
    block_rows = math.gcd(row_count, key_block_rows)

    def advance(counter, state):
        block_start = counter * block_rows
        key_block = lax.dynamic_slice_in_dim(gathered[0], block_start, block_rows, 0)
        rows_here = 0 + block_start + jnp.arange(block_rows, dtype=jnp.int32)
        key_mask = (rows_here < prompt_limit)[None, :]
        return add_stats(state, key_block, key_mask)

    running = lax.fori_loop(0, row_count // block_rows, advance, running)
    log_total = running[0] + jnp.log(running[1])
    row_count = gathered.shape[1]
    prompt_block_rows = math.gcd(row_count, key_block_rows)

    def advance(counter, state):
        block_start = counter * prompt_block_rows
        key_block = lax.dynamic_slice_in_dim(gathered[0], block_start, prompt_block_rows, 0)
        value_block = lax.dynamic_slice_in_dim(gathered[1], block_start, prompt_block_rows, 0)
        rows_here = 0 + block_start + jnp.arange(prompt_block_rows, dtype=jnp.int32)
        key_mask = (rows_here < prompt_limit)[None, :]
        query_part, key_part, value_part = block_grads(key_block, value_block, key_mask, log_total)
        update = jnp.stack([key_part, value_part])
        written = lax.dynamic_update_slice_in_dim(state[1], update, 0 + block_start, 1)
        return (state[0] + query_part, written)

    query_sum, key_value_sum = lax.fori_loop(0, row_count // prompt_block_rows, advance, empty)
    prompt_value_sum = jnp.sum(key_value_sum[1], axis=0)
    summed = lax.psum_scatter(key_value_sum, "reply", scatter_dimension=1, tiled=True)
    query_part, key_part, value_part = block_grads(own_keys, own_values, causal, log_total)
    query_grad = ((query_sum + query_part) * factor).astype(jnp.bfloat16)
    query_grad = query_grad.reshape(1, 1, row_total, shared * head_size)
    reply_grad = jnp.stack([key_part, value_part]).astype(jnp.bfloat16)[None, None]
    bias_term = prompt_value_sum + jnp.sum(value_part, axis=0)
    value_bias = lax.psum(bias_term, ("grp", "reply"))
    prompt_grad = summed.astype(jnp.bfloat16)[None]
    return (query_grad, reply_grad, prompt_grad, value_bias)


def solution(mesh):
    in_specs = (
        P("grp", "reply", None, "head"),
        P("grp", "reply", None, None, "head"),
        P("grp", None, "reply", "head"),
        P("grp", "reply", None, "head"),
        P("grp", "reply", None, "head"),
        P("grp"),
        P("grp", "reply"),
    )
    out_specs = (
        P("grp", "reply", None, "head"),
        P("grp", "reply", None, None, "head"),
        P("grp", None, "reply", "head"),
        P("head"),
    )
    return jax.shard_map(
        on_device, mesh=mesh, in_specs=in_specs, out_specs=out_specs, check_vma=False
    )
```

profile of v0, /device:TPU:64, one launch (start us, length us, event | category | flops | bytes accessed | tf_op | source)
XLA Modules:
  0.0 473.6 jit_solution(14809020102475673221)
XLA Ops:
  8.0 1.2 copy.20
  9.5 46.4 %all-gather = bf16[1,2,1024,128]{3,2,1,0:T(8,128)(2,1)S(1)} all-gather(bf16[1,2,64,128]{3,2,1,0:T(8,128)(2,1)S(1)} %copy-done.6), channel_id=2, replica_groups=mesh['grp'=8,'reply'=16,'head'=4] {'reply'}, dimensions={2}, use_global_device_ids=true | all-gather | bytes 557056 | tf_op jit(solution)/shard_map/all_gather | solution.py:84
  56.0 0.9 copy.50
  56.9 1.2 copy.23
  58.1 1.3 bitcast_convert_fusion
  59.4 2.7 copy.41
  62.0 1.6 multiply_reduce_fusion
  63.7 1.3 copy.25
  65.0 0.5 fusion.42
  65.5 1.3 copy-done
  67.2 6.8 %while.31 = (s32[]{:T(128)}, f32[8,256]{1,0:T(8,128)S(1)}, f32[8,256]{1,0:T(8,128)S(1)}, s32[]{:T(128)}, bf16[2,1024,128]{2,1,0:T(8,128)(2,1)S(1)}, /*index=5*/b...) while((s32[]{:T(128)}, f32[8,256]{1,0:T(8,128)S(1)}, f32[8,256]{1,0:T(8,128)S(1)}, ...), condition=%wide.region_5.6_spmd, body=%wide.region_2.5_spmd.sunk | while | flops 137892352 | bytes 5416095 | solution.py:95
  67.2 0.7 add_compare_fusion.4
  67.9 0.4 bitcast_reduce_fusion.2
  68.3 0.5 fusion.75
  68.9 0.7 add_compare_fusion.4
  69.6 0.5 bitcast_reduce_fusion.2
  70.0 0.5 fusion.75
  70.6 0.7 add_compare_fusion.4
  71.3 0.5 bitcast_reduce_fusion.2
  71.7 0.5 fusion.75
  72.3 0.7 add_compare_fusion.4
  73.0 0.5 bitcast_reduce_fusion.2
  73.5 0.5 fusion.75
  74.0 1.1 broadcast_in_dim.120
  75.1 15.3 %while.32 = (s32[]{:T(128)}, f32[256,8,128]{0,2,1:T(8,128)S(1)}, f32[2,1024,128]{2,1,0:T(8,128)}, bf16[2,1024,128]{2,1,0:T(8,128)(2,1)S(1)}, s32[]{:T(128)}, /*i...) while((s32[]{:T(128)}, f32[256,8,128]{0,2,1:T(8,128)S(1)}, ...), condition=%wide.region_7.8_spmd.clone, body=%wide.region_6.7_spmd.clone.sunk | while | flops 675381760 | bytes 15680469 | solution.py:111
  75.1 0.7 add_compare_fusion.5
  75.8 0.6 fusion.87
  76.4 0.4 convolution_bitcast_fusion.7
  76.8 0.4 fusion.88
  77.2 0.4 fusion.90
  77.7 0.5 fusion.89
  78.2 0.7 maximum_dynamic-update-slice_fusion.2
  78.9 0.7 add_compare_fusion.5
  79.6 0.6 fusion.87
  80.2 0.4 convolution_bitcast_fusion.7
  80.6 0.4 fusion.88
  81.1 0.4 fusion.90
  81.5 0.5 fusion.89
  82.0 0.7 maximum_dynamic-update-slice_fusion.2
  82.7 0.7 add_compare_fusion.5
  83.4 0.6 fusion.87
  84.0 0.4 convolution_bitcast_fusion.7
  84.5 0.4 fusion.88
  84.9 0.4 fusion.90
  85.4 0.5 fusion.89
  85.8 0.7 maximum_dynamic-update-slice_fusion.2
  86.6 0.7 add_compare_fusion.5
  87.3 0.6 fusion.87
  87.8 0.4 convolution_bitcast_fusion.7
  88.3 0.4 fusion.88
  88.7 0.4 fusion.90
  89.2 0.5 fusion.89
  89.7 0.7 maximum_dynamic-update-slice_fusion.2
  90.4 1.3 select_bitcast_fusion
  91.8 0.3 copy-done.1
  92.2 0.5 fusion.23
  92.7 1.2 fusion.27
  93.9 2.0 copy.32
  95.9 1.2 slice_reduce_fusion
  97.1 2.0 fusion.41
  99.2 365.0 %psum.7 = f32[128]{0:T(128)} all-reduce(f32[128]{0:T(128)S(1)} %add.113), channel_id=1, replica_groups=mesh['grp'=8,'reply'=16,'head'=4] {'grp','reply'}, use_global_device_ids=true, to_apply=%region_11.12 | all-reduce | flops 128 | bytes 1024 | tf_op jit(solution)/shard_map/psum | solution.py:119
  464.2 0.4 fusion.30
  464.7 0.7 pad_maximum_fusion
  465.3 1.5 convert_bitcast_fusion.1
  (46 shorter events, 1.2 us)
Async XLA Ops:
  7.2 2.4 copy-start.6
  7.2 48.8 %copy-start.4 = (bf16[1,1,256,1024]{3,2,1,0:T(8,128)(2,1)S(1)}, bf16[1,1,256,1024]{3,2,1,0:T(8,128)(2,1)}, u32[]{:S(2)}) copy-start(bf16[1,1,256,1024]{3,2,1,0:T(8,128)(2,1)} %param.14) | copy-start | bytes 1572868
  7.2 458.1 %reduce-scatter.2.cloned.1.call-start = ((), (), s32[]{:S(2)}) async-start(), calls=%async_computation.1 | async-start | bytes 1114112 | tf_op jit(solution)/shard_map/reduce_scatter | solution.py:113
  59.4 2.7 copy-start.3
  59.4 5.6 %copy-start.5 = (bf16[1,1,2,256,128]{4,3,2,1,0:T(8,128)(2,1)S(1)}, bf16[1,1,2,256,128]{4,3,2,1,0:T(8,128)(2,1)}, u32[]{:S(2)}) copy-start(bf16[1,1,2,256,128]{4,3,2,1,0:T(8,128)(2,1)} %param.12) | copy-start | bytes 393220
  65.5 1.4 copy-start
  90.4 1.7 copy-start.1
  92.7 4.4 copy-start.2
Sparse Core Ops, SparseCore 0:
  90.5 87.3 reduce-scatter.1
where the time goes:
time: 475 us; the launch traced here: 474 us
  blocking collectives  411 us (87%)
  other arithmetic  17.9 us (4%)
  matrix products  15.9 us (3%)
  between operations  14.9 us (3%)
  local copies, waits for them, and re-layouts  12.8 us (3%)
    psum x1, blocking collectives, on_device(): value_bias = lax.psum(bias_term, ('grp', 'reply'))  365 us
    all_gather x1, blocking collectives, on_device(): gathered = lax.all_gather(columns, 'reply', axis=1, tiled=True)  46.4 us
    unnamed x22, local copies, waits for them, and re-layouts  11.5 us
  transfers between devices with their start and end apart: 1, of which 0 were waited for; matrix products, arithmetic and copies ran while one was open for 2% of the time, Pallas kernels for 0%

commit v1 on v0

v1 whole, which is shorter than its diff:
```python
import functools
import math

import jax
import jax.numpy as jnp
from jax import lax
from jax.experimental import pallas as pl
from jax.experimental.pallas import tpu as pltpu
from jax.sharding import PartitionSpec as P

NEGATIVE = -1e30
XS = 4
ZS = 4
HD = 128
HEADS = 8
ROWS = 256
SLICE = 64
BLOCK = ZS * SLICE
OWN, LEFT, RIGHT, FAR, REPLY = 0, 1, 2, 3, 4
NT = (((1,), (1,)), ((), ()))
NN = (((1,), (0,)), ((), ()))


def dot(a, b, dims=NN):
    return lax.dot_general(a, b, dims, preferred_element_type=jnp.float32)


def kernel(
    groups,
    plen_ref, rlen_ref, q_hbm, rkv_hbm, pkv_hbm, o_hbm, do_hbm,
    qg_hbm, rg_hbm, pg_hbm, bias_out,
    q_v, do_v, o_v, rkv, kv, probs, dps, dscores, keys_t,
    tops, totals, factors, rowdots, part_k, part_v,
    far_out, far_in, near_out, near_in, col_out, col_in,
    bias_z, bias_x, bias_y, bias_in, qg_v, rg_v, pg_v,
    local_sem, out_sem, z_send, z_recv, x_send, x_recv, relay_send, relay_recv,
    far_send, far_recv, near_send, near_recv, col_send, col_recv,
    bz_send, bz_recv, bx_send, bx_recv, by_send, by_recv,
):
    group = lax.axis_index("grp")
    reply = lax.axis_index("reply")
    x = reply // ZS
    z = reply % ZS
    scale = HD ** (-0.5)
    to_log2 = scale * math.log2(math.e)
    steps = groups.bit_length() - 1

    def at_z(d):
        return {"reply": x * ZS + (z + d) % ZS}

    def at_x(d):
        return {"reply": ((x + d) % XS) * ZS + z}

    def across(i):
        bit = 1 << i
        return {"grp": group + bit - 2 * bit * ((group // bit) % 2)}

    def remote(src, dst, send, recv, device):
        return pltpu.make_async_remote_copy(
            src_ref=src, dst_ref=dst, send_sem=send, recv_sem=recv,
            device_id=device, device_id_type=pl.DeviceIdType.MESH,
        )

    barrier = pltpu.get_barrier_semaphore()
    partners = [at_z(d) for d in range(1, ZS)] + [at_x(d) for d in range(1, XS)]
    partners += [across(i) for i in range(steps)]
    for device in partners:
        pl.semaphore_signal(barrier, inc=1, device_id=device, device_id_type=pl.DeviceIdType.MESH)

    def rows_of(d):
        return pl.ds(pl.multiple_of(((z + d) % ZS) * SLICE, SLICE), SLICE)

    loads = [
        pltpu.make_async_copy(pkv_hbm.at[0], kv.at[x, :, rows_of(0)], local_sem.at[0]),
        pltpu.make_async_copy(do_hbm.at[0, 0], do_v, local_sem.at[1]),
        pltpu.make_async_copy(o_hbm.at[0, 0], o_v, local_sem.at[2]),
        pltpu.make_async_copy(rkv_hbm.at[0, 0], rkv, local_sem.at[3]),
        pltpu.make_async_copy(q_hbm.at[0, 0], q_v, local_sem.at[4]),
    ]
    for load in loads:
        load.start()
    pl.semaphore_wait(barrier, len(partners))

    sends = []

    def start(copy):
        copy.start()
        sends.append(copy)

    def slice_to_neighbours(d, src):
        place = kv.at[x, :, rows_of(-d)]
        for side, way in ((0, 1), (1, -1)):
            start(remote(src, place, x_send.at[side, d], x_recv.at[side, d], at_x(way)))

    for d in range(1, ZS):
        start(remote(pkv_hbm.at[0], kv.at[x, :, rows_of(0)], z_send.at[d], z_recv.at[d], at_z(d)))
    slice_to_neighbours(0, pkv_hbm.at[0])

    def arrived(place, send, recv, device):
        remote(place, place, send, recv, device).wait_recv()

    limit = rlen_ref[0, 0]
    live = lax.broadcasted_iota(jnp.int32, (ROWS, HD), 0) < limit
    ones = jnp.ones((8, HD), jnp.bfloat16)
    loads[1].wait()
    loads[2].wait()
    bias = jnp.zeros((8, HD), jnp.float32)
    for j in range(HEADS):
        cols = slice(j * HD, (j + 1) * HD)
        grad = jnp.where(live, do_v[:, cols].astype(jnp.float32), 0.0)
        do_v[:, cols] = grad.astype(jnp.bfloat16)
        bias = bias + jnp.sum(grad.reshape(ROWS // 8, 8, HD), axis=0)
        product = grad * o_v[:, cols].astype(jnp.float32)
        high = product.astype(jnp.bfloat16)
        low = (product - high.astype(jnp.float32)).astype(jnp.bfloat16)
        rowdots[j] = dot(ones, high, NT) + dot(ones, low, NT)
    bias_z[z] = bias
    for d in range(1, ZS):
        start(remote(bias_z.at[z], bias_z.at[z], bz_send.at[d], bz_recv.at[d], at_z(d)))

    for d in range(1, ZS):
        place = kv.at[x, :, rows_of(-d)]
        arrived(place, z_send.at[d], z_recv.at[d], at_z(d))
        slice_to_neighbours(d, place)

    def first_pass(slot, key, value, visible):
        for j in range(HEADS):
            cols = slice(j * HD, (j + 1) * HD)
            lanes = slice(j * ROWS, (j + 1) * ROWS)
            logits = jnp.where(visible, dot(key, q_v[:, cols], NT) * to_log2, NEGATIVE)
            top = jnp.max(logits, axis=0, keepdims=True)
            power = jnp.exp2(logits - top)
            probs[slot, :, lanes] = power
            tops[slot, j : j + 1, :] = top
            totals[slot, j : j + 1, :] = jnp.sum(power, axis=0, keepdims=True)
            dps[slot, :, lanes] = dot(value, do_v[:, cols], NT) - rowdots[j, 0:1, :]
        columns = slice(slot * BLOCK, (slot + 1) * BLOCK)
        keys_t[:, columns] = key.astype(jnp.float32).T.astype(jnp.bfloat16)

    key_row = lax.broadcasted_iota(jnp.int32, (BLOCK, ROWS), 0)
    prompt_limit = plen_ref[0]

    def prompt_pass(slot, way):
        owner = (x + way) % XS
        first_pass(slot, kv[owner, 0], kv[owner, 1], key_row + owner * BLOCK < prompt_limit)

    loads[3].wait()
    loads[4].wait()
    query_row = lax.broadcasted_iota(jnp.int32, (ROWS, ROWS), 1)
    first_pass(REPLY, rkv[0], rkv[1], key_row <= query_row)

    for d in range(1, ZS):
        there = bias_z.at[(z - d) % ZS]
        arrived(there, bz_send.at[d], bz_recv.at[d], at_z(d))
    bias_x[x] = (bias_z[0] + bias_z[1]) + (bias_z[2] + bias_z[3])
    for d in range(1, XS):
        start(remote(bias_x.at[x], bias_x.at[x], bx_send.at[d], bx_recv.at[d], at_x(d)))

    loads[0].wait()
    prompt_pass(OWN, 0)

    for side, way in ((0, -1), (1, 1)):
        owner = (x + way) % XS
        for d in range(ZS):
            place = kv.at[owner, :, rows_of(-d)]
            arrived(place, x_send.at[side, d], x_recv.at[side, d], at_x(way))
        place = kv.at[owner, side]
        start(remote(place, place, relay_send.at[side], relay_recv.at[side], at_x(-way)))

    for d in range(1, XS):
        there = bias_x.at[(x - d) % XS]
        arrived(there, bx_send.at[d], bx_recv.at[d], at_x(d))
    bias_y[0] = (bias_x[0] + bias_x[1]) + (bias_x[2] + bias_x[3])

    def send_bias(i):
        start(remote(bias_y.at[i], bias_in.at[i], by_send.at[i], by_recv.at[i], across(i)))

    def add_bias(i):
        arrived(bias_in.at[i], by_send.at[i], by_recv.at[i], across(i))
        bias_y[i + 1] = bias_y[i] + bias_in[i]
        if i + 1 < steps:
            send_bias(i + 1)

    if steps > 0:
        send_bias(0)
    prompt_pass(LEFT, -1)
    if steps > 0:
        add_bias(0)
    prompt_pass(RIGHT, 1)
    if steps > 1:
        add_bias(1)
    far = (x + 2) % XS
    for side in (0, 1):
        place = kv.at[far, side]
        arrived(place, relay_send.at[side], relay_recv.at[side], at_x(1))
    prompt_pass(FAR, 2)

    top = jnp.max(tops[...], axis=0)
    total = jnp.zeros((HEADS, ROWS), jnp.float32)
    for slot in range(5):
        total = total + totals[slot] * jnp.exp2(tops[slot] - top)
    for slot in range(5):
        factors[slot] = jnp.exp2(tops[slot] - top) / total

    def second_pass(slot):
        key_part = jnp.zeros((BLOCK, HD), jnp.float32)
        value_part = jnp.zeros((BLOCK, HD), jnp.float32)
        for j in range(HEADS):
            cols = slice(j * HD, (j + 1) * HD)
            lanes = slice(j * ROWS, (j + 1) * ROWS)
            prob = probs[slot, :, lanes] * factors[slot, j : j + 1, :]
            score = (prob * dps[slot, :, lanes]).astype(jnp.bfloat16)
            dscores[slot * BLOCK : (slot + 1) * BLOCK, lanes] = score
            value_part = value_part + dot(prob.astype(jnp.bfloat16), do_v[:, cols])
            key_part = key_part + dot(score, q_v[:, cols])
        return key_part * scale, value_part

    for side, part in enumerate(second_pass(FAR)):
        far_out[side] = part.astype(jnp.bfloat16)
        start(remote(far_out.at[side], far_in.at[side], far_send.at[side], far_recv.at[side],
                     at_x(1 - 2 * side)))
    for side, slot in ((0, RIGHT), (1, LEFT)):
        parts = list(second_pass(slot))
        way = 1 - 2 * side
        arrived(far_in.at[side], far_send.at[side], far_recv.at[side], at_x(way))
        parts[side] = parts[side] + far_in[side].astype(jnp.float32)
        near_out[side, 0] = parts[0].astype(jnp.bfloat16)
        near_out[side, 1] = parts[1].astype(jnp.bfloat16)
        start(remote(near_out.at[side], near_in.at[side], near_send.at[side], near_recv.at[side],
                     at_x(way)))
    part_k[...], part_v[...] = second_pass(OWN)
    if steps > 2:
        add_bias(2)
    bias_out[...] = jnp.sum(bias_y[steps], axis=0, keepdims=True)
    key_part, value_part = second_pass(REPLY)
    rg_v[0] = key_part.astype(jnp.bfloat16)
    rg_v[1] = value_part.astype(jnp.bfloat16)
    reply_store = pltpu.make_async_copy(rg_v, rg_hbm.at[0, 0], out_sem.at[0])
    reply_store.start()

    for side in (0, 1):
        arrived(near_in.at[side], near_send.at[side], near_recv.at[side], at_x(1 - 2 * side))
    for side, part in ((0, part_k), (1, part_v)):
        both = near_in[0, side].astype(jnp.float32) + near_in[1, side].astype(jnp.float32)
        part[...] = part[...] + both
        col_out[side] = part[...].astype(jnp.bfloat16)
    for d in range(1, ZS):
        start(remote(col_out.at[:, rows_of(d)], col_in.at[d], col_send.at[d], col_recv.at[d],
                     at_z(d)))

    for j in range(HEADS):
        cols = slice(j * HD, (j + 1) * HD)
        lanes = slice(j * ROWS, (j + 1) * ROWS)
        turned = dot(keys_t[...], dscores[:, lanes])
        qg_v[:, cols] = (turned.T * scale).astype(jnp.bfloat16)
    query_store = pltpu.make_async_copy(qg_v, qg_hbm.at[0, 0], out_sem.at[1])
    query_store.start()

    for d in range(1, ZS):
        arrived(col_in.at[d], col_send.at[d], col_recv.at[d], at_z(d))
    for side, part in ((0, part_k), (1, part_v)):
        total = part[rows_of(0), :]
        for d in range(1, ZS):
            total = total + col_in[d, side].astype(jnp.float32)
        pg_v[side] = total.astype(jnp.bfloat16)
    prompt_store = pltpu.make_async_copy(pg_v, pg_hbm.at[0], out_sem.at[2])
    prompt_store.start()
    for copy in sends:
        copy.wait_send()
    reply_store.wait()
    query_store.wait()
    prompt_store.wait()


def on_device(groups, queries, reply_kv, prompt_kv, saved_out, grad_out, prompt_len, reply_len):
    half, full = jnp.bfloat16, jnp.float32
    vmem = pltpu.VMEM
    dma = pltpu.SemaphoreType.DMA
    anywhere = pl.BlockSpec(memory_space=pl.ANY)
    smem = pl.BlockSpec(memory_space=pltpu.SMEM)
    steps = groups.bit_length() - 1
    wide = HEADS * HD
    lanes = HEADS * ROWS
    query_grad, reply_grad, prompt_grad, bias = pl.pallas_call(
        functools.partial(kernel, groups),
        out_shape=(
            jax.ShapeDtypeStruct(queries.shape, half),
            jax.ShapeDtypeStruct(reply_kv.shape, half),
            jax.ShapeDtypeStruct(prompt_kv.shape, half),
            jax.ShapeDtypeStruct((1, HD), full),
        ),
        in_specs=[smem, smem] + [anywhere] * 5,
        out_specs=(anywhere, anywhere, anywhere, pl.BlockSpec(memory_space=vmem)),
        scratch_shapes=[
            vmem((ROWS, wide), half),
            vmem((ROWS, wide), half),
            vmem((ROWS, wide), half),
            vmem((2, ROWS, HD), half),
            vmem((XS, 2, BLOCK, HD), half),
            vmem((5, BLOCK, lanes), full),
            vmem((5, BLOCK, lanes), full),
            vmem((5 * BLOCK, lanes), half),
            vmem((HD, 5 * BLOCK), half),
            vmem((5, HEADS, ROWS), full),
            vmem((5, HEADS, ROWS), full),
            vmem((5, HEADS, ROWS), full),
            vmem((HEADS, 8, ROWS), full),
            vmem((BLOCK, HD), full),
            vmem((BLOCK, HD), full),
            vmem((2, BLOCK, HD), half),
            vmem((2, BLOCK, HD), half),
            vmem((2, 2, BLOCK, HD), half),
            vmem((2, 2, BLOCK, HD), half),
            vmem((2, BLOCK, HD), half),
            vmem((ZS, 2, SLICE, HD), half),
            vmem((ZS, 8, HD), full),
            vmem((XS, 8, HD), full),
            vmem((steps + 1, 8, HD), full),
            vmem((max(steps, 1), 8, HD), full),
            vmem((ROWS, wide), half),
            vmem((2, ROWS, HD), half),
            vmem((2, SLICE, HD), half),
            dma((5,)), dma((3,)),
            dma((ZS,)), dma((ZS,)), dma((2, ZS)), dma((2, ZS)), dma((2,)), dma((2,)),
            dma((2,)), dma((2,)), dma((2,)), dma((2,)), dma((ZS,)), dma((ZS,)),
            dma((ZS,)), dma((ZS,)), dma((XS,)), dma((XS,)),
            dma((max(steps, 1),)), dma((max(steps, 1),)),
        ],
        compiler_params=pltpu.CompilerParams(
            collective_id=0, has_side_effects=True, vmem_limit_bytes=56 * 2**20
        ),
        cost_estimate=pl.CostEstimate(
            flops=5 * 2 * lanes * 5 * BLOCK * HD,
            bytes_accessed=5 * 2**20,
            transcendentals=lanes * 5 * BLOCK,
        ),
    )(prompt_len, reply_len, queries, reply_kv, prompt_kv, saved_out, grad_out)
    return query_grad, reply_grad, prompt_grad, bias.reshape(HD)


def solution(mesh):
    in_specs = (
        P("grp", "reply", None, "head"),
        P("grp", "reply", None, None, "head"),
        P("grp", None, "reply", "head"),
        P("grp", "reply", None, "head"),
        P("grp", "reply", None, "head"),
        P("grp"),
        P("grp", "reply"),
    )
    out_specs = (
        P("grp", "reply", None, "head"),
        P("grp", "reply", None, None, "head"),
        P("grp", None, "reply", "head"),
        P("head"),
    )
    return jax.shard_map(
        functools.partial(on_device, mesh.shape["grp"]),
        mesh=mesh, in_specs=in_specs, out_specs=out_specs, check_vma=False,
    )
```

time: 475 us -> 47 us (0.10)
  the two profiles are of different devices: /device:TPU:64 before, /device:TPU:8 now
where the time goes in v1:
time: 47 us; the launch traced here: 46.8 us
  Pallas kernels  41 us (87%)
  local copies, waits for them, and re-layouts  3.84 us (8%)
  between operations  1.94 us (4%)
    pallas_call x1, Pallas kernels, on_device(): pl.pallas_call(functools.partial(kernel, groups), out_shape=(jax.ShapeDty...  41 us
    unnamed x10, local copies, waits for them, and re-layouts  3.84 us

profile of v1, /device:TPU:8, one launch (start us, length us, event | category | flops | bytes accessed | tf_op | source)
XLA Modules:
  0.0 46.8 jit_solution(17866677017757333340)
XLA Ops:
  1.9 41.0 %shard_map.102 = (bf16[1,1,256,1024]{3,2,1,0:T(8,128)(2,1)}, bf16[1,1,2,256,128]{4,3,2,1,0:T(8,128)(2,1)}, bf16[1,2,64,128]{3,2,1,0:T(8,128)(2,1)}, f32[1,128]{1,0:T(1,128)}) custom-call(s32[1]{0:T(128)S(6)} %copy.15.plen_ref, s32[1,1]{1,0:T(1,128)S(6)} %copy.16.rlen_ref, bf16[1,1,256,1024]{3,2,1,0:T(8,128)(2,1)} %q_hbm.1, ...), custom_call_target="tpu_custom_call" | custom-call | flops 3355443200 | bytes 5242880 | tf_op jit(solution)/shard_map/pallas_call | solution.py:284
  42.9 0.0 copy-start
  42.9 1.9 %copy.17 = bf16[1,1,256,1024]{3,2,1,0:T(8,128)(2,1)} copy(bf16[1,1,256,1024]{3,2,1,0:T(8,128)(2,1)} %get-tuple-element.16) | data formatting | bytes 1048576
  44.9 0.0 copy-done
  44.9 0.0 copy-start.1
  44.9 0.7 %copy.18 = bf16[1,1,2,256,128]{4,3,2,1,0:T(8,128)(2,1)} copy(bf16[1,1,2,256,128]{4,3,2,1,0:T(8,128)(2,1)S(1)} %copy-done) | data formatting | bytes 262144
  45.5 0.1 copy-done.1
  45.6 0.0 copy-start.2
  45.6 0.6 %copy.19 = bf16[1,2,64,128]{3,2,1,0:T(8,128)(2,1)} copy(bf16[1,2,64,128]{3,2,1,0:T(8,128)(2,1)S(1)} %copy-done.1) | data formatting | bytes 65536
  46.2 0.0 copy-done.2
  46.3 0.5 %copy.20 = f32[128]{0:T(128)} copy(f32[128]{0:T(128)S(1)} %bitcast.1) | data formatting | bytes 1024
Async XLA Ops:
  42.9 1.9 %copy-start = (bf16[1,1,2,256,128]{4,3,2,1,0:T(8,128)(2,1)S(1)}, bf16[1,1,2,256,128]{4,3,2,1,0:T(8,128)(2,1)}, u32[]{:S(2)}) copy-start(bf16[1,1,2,256,128]{4,3,2,1,0:T(8,128)(2,1)} %get-tuple-element.17) | copy-start | bytes 393220
  44.9 0.8 %copy-start.1 = (bf16[1,2,64,128]{3,2,1,0:T(8,128)(2,1)S(1)}, bf16[1,2,64,128]{3,2,1,0:T(8,128)(2,1)}, u32[]{:S(2)}) copy-start(bf16[1,2,64,128]{3,2,1,0:T(8,128)(2,1)} %get-tuple-element.18) | copy-start | bytes 98308
  45.6 0.7 %copy-start.2 = (f32[1,128]{1,0:T(1,128)S(1)}, f32[1,128]{1,0:T(1,128)}, u32[]{:S(2)}) copy-start(f32[1,128]{1,0:T(1,128)} %get-tuple-element.11) | copy-start | bytes 1540

commit v2 on v1

v2 whole, which is shorter than its diff:
```python
import functools
import math

import jax
import jax.numpy as jnp
from jax import lax
from jax.experimental import pallas as pl
from jax.experimental.pallas import tpu as pltpu
from jax.sharding import PartitionSpec as P

NEGATIVE = -1e30
XS = 4
ZS = 4
HD = 128
HEADS = 8
ROWS = 256
SLICE = 64
BLOCK = ZS * SLICE
NT = (((1,), (1,)), ((), ()))
NN = (((1,), (0,)), ((), ()))


def dot(a, b, dims=NN):
    return lax.dot_general(a, b, dims, preferred_element_type=jnp.float32)


def kernel(
    groups,
    plen_ref, rlen_ref, q_hbm, rkv_hbm, pkv_hbm, o_hbm, do_hbm,
    qg_hbm, rg_hbm, pg_hbm, bias_out,
    q_v, do_v, o_v, kv, mask, probs, dps, dscores, keys_t,
    tops, totals, factors, rowdots, parts,
    far_out, far_in, near_out, near_in, col_out, col_in,
    bias_z, bias_x, bias_y, bias_in, qg_v, rg_v, pg_v,
    local_sem, out_sem, z_send, z_recv, x_send, x_recv, relay_send, relay_recv,
    far_send, far_recv, near_send, near_recv, col_send, col_recv,
    bz_send, bz_recv, bx_send, bx_recv, by_send, by_recv,
):
    group = lax.axis_index("grp")
    reply = lax.axis_index("reply")
    x = reply // ZS
    z = reply % ZS
    scale = HD ** (-0.5)
    to_log2 = scale * math.log2(math.e)
    steps = groups.bit_length() - 1

    def at_z(d):
        return {"reply": x * ZS + (z + d) % ZS}

    def at_x(d):
        return {"reply": ((x + d) % XS) * ZS + z}

    def across(i):
        bit = 1 << i
        return {"grp": group + bit - 2 * bit * ((group // bit) % 2)}

    def remote(src, dst, send, recv, device):
        return pltpu.make_async_remote_copy(
            src_ref=src, dst_ref=dst, send_sem=send, recv_sem=recv,
            device_id=device, device_id_type=pl.DeviceIdType.MESH,
        )

    def arrived(place, send, recv, device):
        remote(place, place, send, recv, device).wait_recv()

    def rows_of(d):
        return pl.ds(pl.multiple_of(((z + d) % ZS) * SLICE, SLICE), SLICE)

    barrier = pltpu.get_barrier_semaphore()
    partners = [at_z(d) for d in range(1, ZS)] + [at_x(d) for d in range(1, XS)]
    partners += [across(i) for i in range(steps)]
    for device in partners:
        pl.semaphore_signal(barrier, inc=1, device_id=device, device_id_type=pl.DeviceIdType.MESH)

    loads = [
        pltpu.make_async_copy(pkv_hbm.at[0], kv.at[x, :, rows_of(0)], local_sem.at[0]),
        pltpu.make_async_copy(do_hbm.at[0, 0], do_v, local_sem.at[1]),
        pltpu.make_async_copy(o_hbm.at[0, 0], o_v, local_sem.at[2]),
        pltpu.make_async_copy(rkv_hbm.at[0, 0], kv.at[XS], local_sem.at[3]),
        pltpu.make_async_copy(q_hbm.at[0, 0], q_v, local_sem.at[4]),
    ]
    for load in loads:
        load.start()
    pl.semaphore_wait(barrier, len(partners))

    own = kv.at[x, :, rows_of(0)]

    def z_copy(d):
        return remote(pkv_hbm.at[0], own, z_send.at[d], z_recv.at[d], at_z(d))

    def x_copy(side, d):
        place = kv.at[x, :, rows_of(-d)]
        src = pkv_hbm.at[0] if d == 0 else place
        return remote(src, place, x_send.at[side, d], x_recv.at[side, d], at_x(1 - 2 * side))

    def relay_copy(side):
        way = 1 - 2 * side
        place = kv.at[(x - way) % XS, side]
        return remote(place, place, relay_send.at[side], relay_recv.at[side], at_x(way))

    def far_copy(side):
        return remote(far_out.at[side], far_in.at[side], far_send.at[side], far_recv.at[side],
                      at_x(1 - 2 * side))

    def near_copy(side):
        return remote(near_out.at[side], near_in.at[side], near_send.at[side], near_recv.at[side],
                      at_x(1 - 2 * side))

    def col_copy(d):
        return remote(col_out.at[:, rows_of(d)], col_in.at[d], col_send.at[d], col_recv.at[d],
                      at_z(d))

    def bz_copy(d):
        return remote(bias_z.at[z], bias_z.at[z], bz_send.at[d], bz_recv.at[d], at_z(d))

    def bx_copy(d):
        return remote(bias_x.at[x], bias_x.at[x], bx_send.at[d], bx_recv.at[d], at_x(d))

    def by_copy(i):
        return remote(bias_y.at[i], bias_in.at[i], by_send.at[i], by_recv.at[i], across(i))

    for d in range(1, ZS):
        z_copy(d).start()
    for side in (0, 1):
        x_copy(side, 0).start()

    for i in (1, 2):
        loads[i].wait()
    limit = rlen_ref[...]
    live = lax.broadcasted_iota(jnp.int32, (ROWS, HD), 0) < limit
    ones = jnp.ones((8, HD), jnp.bfloat16)
    bias = jnp.zeros((8, HD), jnp.float32)
    for j in range(HEADS):
        cols = slice(j * HD, (j + 1) * HD)
        grad = jnp.where(live, do_v[:, cols].astype(jnp.float32), 0.0)
        do_v[:, cols] = grad.astype(jnp.bfloat16)
        bias = bias + jnp.sum(grad.reshape(ROWS // 8, 8, HD), axis=0)
        product = grad * o_v[:, cols].astype(jnp.float32)
        high = product.astype(jnp.bfloat16)
        low = (product - high.astype(jnp.float32)).astype(jnp.bfloat16)
        rowdots[j] = dot(ones, high, NT) + dot(ones, low, NT)
    bias_z[z] = bias
    for d in range(1, ZS):
        bz_copy(d).start()

    for d in range(1, ZS):
        arrived(kv.at[x, :, rows_of(-d)], z_send.at[d], z_recv.at[d], at_z(d))
        for side in (0, 1):
            x_copy(side, d).start()

    for i in (0, 3, 4):
        loads[i].wait()
    prompt_limit = plen_ref[...]
    key_row = lax.broadcasted_iota(jnp.int32, (BLOCK, ROWS), 0)
    query_row = lax.broadcasted_iota(jnp.int32, (BLOCK, ROWS), 1)

    def add_bias(i):
        arrived(bias_in.at[i], by_send.at[i], by_recv.at[i], across(i))
        bias_y[i + 1] = bias_y[i] + bias_in[i]
        if i + 1 < steps:
            by_copy(i + 1).start()

    def first_pass(step, carry):
        @pl.when(step == 1)
        def _():
            for d in range(1, ZS):
                arrived(bias_z.at[(z - d) % ZS], bz_send.at[d], bz_recv.at[d], at_z(d))
            bias_x[x] = (bias_z[0] + bias_z[1]) + (bias_z[2] + bias_z[3])
            for d in range(1, XS):
                bx_copy(d).start()

        @pl.when(step == 2)
        def _():
            for side in (0, 1):
                way = 1 - 2 * side
                for d in range(ZS):
                    arrived(kv.at[(x - way) % XS, :, rows_of(-d)], x_send.at[side, d],
                            x_recv.at[side, d], at_x(way))
                relay_copy(side).start()
            for d in range(1, XS):
                arrived(bias_x.at[(x - d) % XS], bx_send.at[d], bx_recv.at[d], at_x(d))
            bias_y[0] = (bias_x[0] + bias_x[1]) + (bias_x[2] + bias_x[3])
            if steps > 0:
                by_copy(0).start()

        @pl.when(step == 3)
        def _():
            if steps > 0:
                add_bias(0)

        @pl.when(step == 4)
        def _():
            for side in (0, 1):
                arrived(kv.at[(x + 2) % XS, side], relay_send.at[side], relay_recv.at[side],
                        at_x(1 - 2 * side))
            if steps > 1:
                add_bias(1)

        from_reply = 1 - (step + 3) // 4
        turn = step + 3 - 4 * ((step + 3) // 4)
        owner = (x + turn + turn // 2 - 2 * (turn // 3)) % XS
        block = from_reply * XS + (1 - from_reply) * owner
        last = from_reply * query_row + (1 - from_reply) * (prompt_limit - 1 - owner * BLOCK)
        mask[...] = jnp.where(key_row <= last, 0.0, NEGATIVE)
        key, value = kv[block, 0], kv[block, 1]
        columns = pl.ds(pl.multiple_of(step * BLOCK, BLOCK), BLOCK)
        keys_t[:, columns] = key.astype(jnp.float32).T.astype(jnp.bfloat16)
        for j in range(HEADS):
            cols = slice(j * HD, (j + 1) * HD)
            lanes = slice(j * ROWS, (j + 1) * ROWS)
            logits = dot(key, q_v[:, cols], NT) * to_log2 + mask[...]
            top = jnp.max(logits, axis=0, keepdims=True)
            power = jnp.exp2(logits - top)
            probs[step, :, lanes] = power
            tops[step, j : j + 1, :] = top
            totals[step, j : j + 1, :] = jnp.sum(power, axis=0, keepdims=True)
            dps[step, :, lanes] = dot(value, do_v[:, cols], NT) - rowdots[j, 0:1, :]
        return carry

    lax.fori_loop(0, 5, first_pass, 0)

    top = jnp.max(tops[...], axis=0)
    total = jnp.zeros((HEADS, ROWS), jnp.float32)
    for slot in range(5):
        total = total + totals[slot] * jnp.exp2(tops[slot] - top)
    for slot in range(5):
        factors[slot] = jnp.exp2(tops[slot] - top) / total

    def second_pass(turn, carry):
        step = 4 - turn
        key_part = jnp.zeros((BLOCK, HD), jnp.float32)
        value_part = jnp.zeros((BLOCK, HD), jnp.float32)
        rows = pl.ds(pl.multiple_of(step * BLOCK, BLOCK), BLOCK)
        for j in range(HEADS):
            cols = slice(j * HD, (j + 1) * HD)
            lanes = slice(j * ROWS, (j + 1) * ROWS)
            prob = probs[step, :, lanes] * factors[step, j : j + 1, :]
            score = (prob * dps[step, :, lanes]).astype(jnp.bfloat16)
            dscores[rows, lanes] = score
            value_part = value_part + dot(prob.astype(jnp.bfloat16), do_v[:, cols])
            key_part = key_part + dot(score, q_v[:, cols])
        parts[step, 0] = key_part * scale
        parts[step, 1] = value_part

        @pl.when(step == 4)
        def _():
            far_out[...] = parts[4].astype(jnp.bfloat16)
            for side in (0, 1):
                far_copy(side).start()

        for side, slot in ((0, 2), (1, 3)):
            @pl.when(step == slot)
            def _():
                arrived(far_in.at[side], far_send.at[side], far_recv.at[side], at_x(1 - 2 * side))
                other = 1 - side
                both = parts[slot, side] + far_in[side].astype(jnp.float32)
                near_out[side, side] = both.astype(jnp.bfloat16)
                near_out[side, other] = parts[slot, other].astype(jnp.bfloat16)
                near_copy(side).start()

        @pl.when(step == 1)
        def _():
            if steps > 2:
                add_bias(2)

        @pl.when(step == 0)
        def _():
            rg_v[...] = parts[0].astype(jnp.bfloat16)
        return carry

    lax.fori_loop(0, 5, second_pass, 0)
    reply_store = pltpu.make_async_copy(rg_v, rg_hbm.at[0, 0], out_sem.at[0])
    reply_store.start()
    bias_out[...] = jnp.sum(bias_y[steps], axis=0, keepdims=True)

    for side in (0, 1):
        arrived(near_in.at[side], near_send.at[side], near_recv.at[side], at_x(1 - 2 * side))
    parts[1] = parts[1] + (near_in[0].astype(jnp.float32) + near_in[1].astype(jnp.float32))
    col_out[...] = parts[1].astype(jnp.bfloat16)
    for d in range(1, ZS):
        col_copy(d).start()

    for j in range(HEADS):
        cols = slice(j * HD, (j + 1) * HD)
        lanes = slice(j * ROWS, (j + 1) * ROWS)
        turned = dot(keys_t[...], dscores[:, lanes])
        qg_v[:, cols] = (turned.T * scale).astype(jnp.bfloat16)
    query_store = pltpu.make_async_copy(qg_v, qg_hbm.at[0, 0], out_sem.at[1])
    query_store.start()

    for d in range(1, ZS):
        arrived(col_in.at[d], col_send.at[d], col_recv.at[d], at_z(d))
    for side in (0, 1):
        total = parts[1, side, rows_of(0), :]
        for d in range(1, ZS):
            total = total + col_in[d, side].astype(jnp.float32)
        pg_v[side] = total.astype(jnp.bfloat16)
    prompt_store = pltpu.make_async_copy(pg_v, pg_hbm.at[0], out_sem.at[2])
    prompt_store.start()
    started = [z_copy(d) for d in range(1, ZS)] + [col_copy(d) for d in range(1, ZS)]
    started += [x_copy(side, d) for side in (0, 1) for d in range(ZS)]
    started += [f(side) for f in (relay_copy, far_copy, near_copy) for side in (0, 1)]
    started += [bz_copy(d) for d in range(1, ZS)] + [bx_copy(d) for d in range(1, XS)]
    started += [by_copy(i) for i in range(steps)]
    for copy in started:
        copy.wait_send()
    reply_store.wait()
    query_store.wait()
    prompt_store.wait()


def hand_over(*refs):
    sem = refs[-1]
    half = (len(refs) - 1) // 2
    copies = [
        pltpu.make_async_copy(src, dst, sem.at[i])
        for i, (src, dst) in enumerate(zip(refs[:half], refs[half : 2 * half]))
    ]
    for copy in copies:
        copy.start()
    for copy in copies:
        copy.wait()


def on_device(groups, queries, reply_kv, prompt_kv, saved_out, grad_out, prompt_len, reply_len):
    half, full = jnp.bfloat16, jnp.float32
    vmem = pltpu.VMEM
    dma = pltpu.SemaphoreType.DMA
    anywhere = pl.BlockSpec(memory_space=pl.ANY)
    steps = groups.bit_length() - 1
    wide = HEADS * HD
    lanes = HEADS * ROWS
    results = pl.pallas_call(
        functools.partial(kernel, groups),
        out_shape=(
            jax.ShapeDtypeStruct(queries.shape, half),
            jax.ShapeDtypeStruct(reply_kv.shape, half),
            jax.ShapeDtypeStruct(prompt_kv.shape, half),
            jax.ShapeDtypeStruct((1, HD), full),
        ),
        in_specs=[pl.BlockSpec(memory_space=vmem)] * 2 + [anywhere] * 5,
        out_specs=(anywhere, anywhere, anywhere, pl.BlockSpec(memory_space=vmem)),
        scratch_shapes=[
            vmem((ROWS, wide), half),
            vmem((ROWS, wide), half),
            vmem((ROWS, wide), half),
            vmem((XS + 1, 2, BLOCK, HD), half),
            vmem((BLOCK, ROWS), full),
            vmem((5, BLOCK, lanes), full),
            vmem((5, BLOCK, lanes), full),
            vmem((5 * BLOCK, lanes), half),
            vmem((HD, 5 * BLOCK), half),
            vmem((5, HEADS, ROWS), full),
            vmem((5, HEADS, ROWS), full),
            vmem((5, HEADS, ROWS), full),
            vmem((HEADS, 8, ROWS), full),
            vmem((5, 2, BLOCK, HD), full),
            vmem((2, BLOCK, HD), half),
            vmem((2, BLOCK, HD), half),
            vmem((2, 2, BLOCK, HD), half),
            vmem((2, 2, BLOCK, HD), half),
            vmem((2, BLOCK, HD), half),
            vmem((ZS, 2, SLICE, HD), half),
            vmem((ZS, 8, HD), full),
            vmem((XS, 8, HD), full),
            vmem((steps + 1, 8, HD), full),
            vmem((max(steps, 1), 8, HD), full),
            vmem((ROWS, wide), half),
            vmem((2, ROWS, HD), half),
            vmem((2, SLICE, HD), half),
            dma((5,)), dma((3,)),
            dma((ZS,)), dma((ZS,)), dma((2, ZS)), dma((2, ZS)), dma((2,)), dma((2,)),
            dma((2,)), dma((2,)), dma((2,)), dma((2,)), dma((ZS,)), dma((ZS,)),
            dma((ZS,)), dma((ZS,)), dma((XS,)), dma((XS,)),
            dma((max(steps, 1),)), dma((max(steps, 1),)),
        ],
        compiler_params=pltpu.CompilerParams(
            collective_id=0, has_side_effects=True, vmem_limit_bytes=56 * 2**20
        ),
        cost_estimate=pl.CostEstimate(
            flops=5 * 2 * lanes * 5 * BLOCK * HD,
            bytes_accessed=5 * 2**20,
            transcendentals=lanes * 5 * BLOCK,
        ),
    )(prompt_len.reshape(1, 1), reply_len, queries, reply_kv, prompt_kv, saved_out, grad_out)
    query_grad, reply_grad, prompt_grad, bias = pl.pallas_call(
        hand_over,
        out_shape=tuple(jax.ShapeDtypeStruct(r.shape, r.dtype) for r in results),
        in_specs=[anywhere] * 4,
        out_specs=(anywhere,) * 4,
        scratch_shapes=[dma((4,))],
        compiler_params=pltpu.CompilerParams(vmem_limit_bytes=60 * 2**20),
    )(*results)
    return query_grad, reply_grad, prompt_grad, bias.reshape(HD)


def solution(mesh):
    in_specs = (
        P("grp", "reply", None, "head"),
        P("grp", "reply", None, None, "head"),
        P("grp", None, "reply", "head"),
        P("grp", "reply", None, "head"),
        P("grp", "reply", None, "head"),
        P("grp"),
        P("grp", "reply"),
    )
    out_specs = (
        P("grp", "reply", None, "head"),
        P("grp", "reply", None, None, "head"),
        P("grp", None, "reply", "head"),
        P("head"),
    )
    return jax.shard_map(
        functools.partial(on_device, mesh.shape["grp"]),
        mesh=mesh, in_specs=in_specs, out_specs=out_specs, check_vma=False,
    )
```

time: 47 us -> 65.6 us (1.40)
  Pallas kernels: 41 us -> 63.5 us
  local copies, waits for them, and re-layouts: 3.84 us -> 0 us
    pallas_call x0 -> x1, Pallas kernels: none -> 22 us  [on_device(): pl.pallas_call(hand_over, out_shape=tuple((jax.ShapeDtypeStruct(r.shape,...]
    unnamed x10 -> x0, local copies, waits for them, and re-layouts: 3.84 us -> none
where the time goes in v2:
time: 65.6 us; the launch traced here: 65.4 us
  Pallas kernels  63.5 us (97%)
  between operations  1.93 us (3%)
    pallas_call x1, Pallas kernels, on_device(): pl.pallas_call(functools.partial(kernel, groups), out_shape=(jax.ShapeDty...  41.5 us
    pallas_call x1, Pallas kernels, on_device(): pl.pallas_call(hand_over, out_shape=tuple((jax.ShapeDtypeStruct(r.shape,...  22 us

profile of v2, /device:TPU:8, one launch (start us, length us, event | category | flops | bytes accessed | tf_op | source)
XLA Modules:
  0.0 65.4 jit_solution(17170031233327350413)
XLA Ops:
  1.9 41.5 %shard_map.102 = (bf16[1,1,256,1024]{3,2,1,0:T(8,128)(2,1)}, bf16[1,1,2,256,128]{4,3,2,1,0:T(8,128)(2,1)}, bf16[1,2,64,128]{3,2,1,0:T(8,128)(2,1)}, f32[1,128]{1,0:T(1,128)}) custom-call(s32[1,1]{1,0:T(1,128)} %bitcast.2.plen_ref, s32[1,1]{1,0:T(1,128)S(6)} %copy.12.rlen_ref, bf16[1,1,256,1024]{3,2,1,0:T(8,128)(2,1)} %q_hbm.1, ...), custom_call_target="tpu_custom_call" | custom-call | flops 3355443200 | bytes 5242880 | tf_op jit(solution)/shard_map/pallas_call | solution.py:333
  43.4 22.0 %shard_map.103 = (bf16[1,1,256,1024]{3,2,1,0:T(8,128)(2,1)}, bf16[1,1,2,256,128]{4,3,2,1,0:T(8,128)(2,1)}, bf16[1,2,64,128]{3,2,1,0:T(8,128)(2,1)}, f32[1,128]{1,0:T(1,128)}) custom-call(bf16[1,1,256,1024]{3,2,1,0:T(8,128)(2,1)} %get-tuple-element.12.refs_0_, bf16[1,1,2,256,128]{4,3,2,1,0:T(8,128)(2,1)} %get-tuple-element.13.refs_1_, ...), custom_call_target="tpu_custom_call" | custom-call | tf_op jit(solution)/shard_map/pallas_call | solution.py:386

commit v3 on v2

--- a/solution.py
+++ b/solution.py
@@ -28,7 +28,7 @@
     groups,
     plen_ref, rlen_ref, q_hbm, rkv_hbm, pkv_hbm, o_hbm, do_hbm,
     qg_hbm, rg_hbm, pg_hbm, bias_out,
-    q_v, do_v, o_v, kv, mask, probs, dps, dscores, keys_t,
+    q_v, do_v, o_v, kv, mask, probs, dscores, keys_t,
     tops, totals, factors, rowdots, parts,
     far_out, far_in, near_out, near_in, col_out, col_in,
     bias_z, bias_x, bias_y, bias_in, qg_v, rg_v, pg_v,
@@ -81,30 +81,49 @@
     ]
     for load in loads:
         load.start()
-    pl.semaphore_wait(barrier, len(partners))
-
-    own = kv.at[x, :, rows_of(0)]
-
-    def z_copy(d):
-        return remote(pkv_hbm.at[0], own, z_send.at[d], z_recv.at[d], at_z(d))
-
-    def x_copy(side, d):
-        place = kv.at[x, :, rows_of(-d)]
-        src = pkv_hbm.at[0] if d == 0 else place
-        return remote(src, place, x_send.at[side, d], x_recv.at[side, d], at_x(1 - 2 * side))
-
-    def relay_copy(side):
+
+    def z_copy(kind, d):
+        place = kv.at[x, kind, rows_of(0)]
+        return remote(place, place, z_send.at[kind, d], z_recv.at[kind, d], at_z(d))
+
+    def z_wait(kind, d):
+        arrived(kv.at[x, kind, rows_of(-d)], z_send.at[kind, d], z_recv.at[kind, d], at_z(d))
+
+    def x_copy(kind, side, d):
+        place = kv.at[x, kind, rows_of(-d)]
+        return remote(place, place, x_send.at[kind, side, d], x_recv.at[kind, side, d],
+                      at_x(1 - 2 * side))
+
+    def x_wait(kind, side):
         way = 1 - 2 * side
-        place = kv.at[(x - way) % XS, side]
-        return remote(place, place, relay_send.at[side], relay_recv.at[side], at_x(way))
+        for d in range(ZS):
+            arrived(kv.at[(x - way) % XS, kind, rows_of(-d)], x_send.at[kind, side, d],
+                    x_recv.at[kind, side, d], at_x(way))
+
+    def half_of(side):
+        return pl.ds(side * (BLOCK // 2), BLOCK // 2)
+
+    def relay_copy(kind, side):
+        way = 1 - 2 * side
+        place = kv.at[(x - way) % XS, kind, half_of(side)]
+        return remote(place, place, relay_send.at[kind, side], relay_recv.at[kind, side],
+                      at_x(way))
+
+    def relay_wait(kind, side):
+        arrived(kv.at[(x + 2) % XS, kind, half_of(side)], relay_send.at[kind, side],
+                relay_recv.at[kind, side], at_x(1 - 2 * side))
 
     def far_copy(side):
         return remote(far_out.at[side], far_in.at[side], far_send.at[side], far_recv.at[side],
                       at_x(1 - 2 * side))
 
-    def near_copy(side):
-        return remote(near_out.at[side], near_in.at[side], near_send.at[side], near_recv.at[side],
-                      at_x(1 - 2 * side))
+    def near_copy(side, d):
+        return remote(near_out.at[side, :, rows_of(d)], near_in.at[side, :, rows_of(d)],
+                      near_send.at[side, d], near_recv.at[side, d], at_x(1 - 2 * side))
+
+    def near_wait(side, d):
+        arrived(near_in.at[side, :, rows_of(d)], near_send.at[side, d], near_recv.at[side, d],
+                at_x(1 - 2 * side))
 
     def col_copy(d):
         return remote(col_out.at[:, rows_of(d)], col_in.at[d], col_send.at[d], col_recv.at[d],
@@ -119,10 +138,13 @@
     def by_copy(i):
         return remote(bias_y.at[i], bias_in.at[i], by_send.at[i], by_recv.at[i], across(i))
 
-    for d in range(1, ZS):
-        z_copy(d).start()
-    for side in (0, 1):
-        x_copy(side, 0).start()
+    loads[0].wait()
+    pl.semaphore_wait(barrier, len(partners))
+    for kind in (0, 1):
+        for d in range(1, ZS):
+            z_copy(kind, d).start()
+        for side in (0, 1):
+            x_copy(kind, side, 0).start()
 
     for i in (1, 2):
         loads[i].wait()
@@ -143,12 +165,14 @@
     for d in range(1, ZS):
         bz_copy(d).start()
 
-    for d in range(1, ZS):
-        arrived(kv.at[x, :, rows_of(-d)], z_send.at[d], z_recv.at[d], at_z(d))
-        for side in (0, 1):
-            x_copy(side, d).start()
-
-    for i in (0, 3, 4):
+    def forward(kind):
+        for d in range(1, ZS):
+            z_wait(kind, d)
+            for side in (0, 1):
+                x_copy(kind, side, d).start()
+
+    forward(0)
+    for i in (3, 4):
         loads[i].wait()
     prompt_limit = plen_ref[...]
     key_row = lax.broadcasted_iota(jnp.int32, (BLOCK, ROWS), 0)
@@ -160,9 +184,16 @@
         if i + 1 < steps:
             by_copy(i + 1).start()
 
+    def source(step):
+        from_reply = 1 - (step + 3) // 4
+        turn = step + 3 - 4 * ((step + 3) // 4)
+        owner = (x + turn + turn // 2 - 2 * (turn // 3)) % XS
+        return from_reply, owner, from_reply * XS + (1 - from_reply) * owner
+
     def first_pass(step, carry):
         @pl.when(step == 1)
         def _():
+            forward(1)
             for d in range(1, ZS):
                 arrived(bias_z.at[(z - d) % ZS], bz_send.at[d], bz_recv.at[d], at_z(d))
             bias_x[x] = (bias_z[0] + bias_z[1]) + (bias_z[2] + bias_z[3])
@@ -172,11 +203,8 @@
         @pl.when(step == 2)
         def _():
             for side in (0, 1):
-                way = 1 - 2 * side
-                for d in range(ZS):
-                    arrived(kv.at[(x - way) % XS, :, rows_of(-d)], x_send.at[side, d],
-                            x_recv.at[side, d], at_x(way))
-                relay_copy(side).start()
+                x_wait(0, side)
+                relay_copy(0, side).start()
             for d in range(1, XS):
                 arrived(bias_x.at[(x - d) % XS], bx_send.at[d], bx_recv.at[d], at_x(d))
             bias_y[0] = (bias_x[0] + bias_x[1]) + (bias_x[2] + bias_x[3])
@@ -185,24 +213,23 @@
 
         @pl.when(step == 3)
         def _():
+            for side in (0, 1):
+                x_wait(1, side)
+                relay_copy(1, side).start()
             if steps > 0:
                 add_bias(0)
 
         @pl.when(step == 4)
         def _():
             for side in (0, 1):
-                arrived(kv.at[(x + 2) % XS, side], relay_send.at[side], relay_recv.at[side],
-                        at_x(1 - 2 * side))
+                relay_wait(0, side)
             if steps > 1:
                 add_bias(1)
 
-        from_reply = 1 - (step + 3) // 4
-        turn = step + 3 - 4 * ((step + 3) // 4)
-        owner = (x + turn + turn // 2 - 2 * (turn // 3)) % XS
-        block = from_reply * XS + (1 - from_reply) * owner
+        from_reply, owner, block = source(step)
         last = from_reply * query_row + (1 - from_reply) * (prompt_limit - 1 - owner * BLOCK)
         mask[...] = jnp.where(key_row <= last, 0.0, NEGATIVE)
-        key, value = kv[block, 0], kv[block, 1]
+        key = kv[block, 0]
         columns = pl.ds(pl.multiple_of(step * BLOCK, BLOCK), BLOCK)
         keys_t[:, columns] = key.astype(jnp.float32).T.astype(jnp.bfloat16)
         for j in range(HEADS):
@@ -214,7 +241,6 @@
             probs[step, :, lanes] = power
             tops[step, j : j + 1, :] = top
             totals[step, j : j + 1, :] = jnp.sum(power, axis=0, keepdims=True)
-            dps[step, :, lanes] = dot(value, do_v[:, cols], NT) - rowdots[j, 0:1, :]
         return carry
 
     lax.fori_loop(0, 5, first_pass, 0)
@@ -226,8 +252,12 @@
     for slot in range(5):
         factors[slot] = jnp.exp2(tops[slot] - top) / total
 
+    for side in (0, 1):
+        relay_wait(1, side)
+
     def second_pass(turn, carry):
         step = 4 - turn
+        value = kv[source(step)[2], 1]
         key_part = jnp.zeros((BLOCK, HD), jnp.float32)
         value_part = jnp.zeros((BLOCK, HD), jnp.float32)
         rows = pl.ds(pl.multiple_of(step * BLOCK, BLOCK), BLOCK)
@@ -235,7 +265,8 @@
             cols = slice(j * HD, (j + 1) * HD)
             lanes = slice(j * ROWS, (j + 1) * ROWS)
             prob = probs[step, :, lanes] * factors[step, j : j + 1, :]
-            score = (prob * dps[step, :, lanes]).astype(jnp.bfloat16)
+            dprob = dot(value, do_v[:, cols], NT) - rowdots[j, 0:1, :]
+            score = (prob * dprob).astype(jnp.bfloat16)
             dscores[rows, lanes] = score
             value_part = value_part + dot(prob.astype(jnp.bfloat16), do_v[:, cols])
             key_part = key_part + dot(score, q_v[:, cols])
@@ -256,12 +287,24 @@
                 both = parts[slot, side] + far_in[side].astype(jnp.float32)
                 near_out[side, side] = both.astype(jnp.bfloat16)
                 near_out[side, other] = parts[slot, other].astype(jnp.bfloat16)
-                near_copy(side).start()
+                for d in (1, 2, 3, 0):
+                    near_copy(side, d).start()
 
         @pl.when(step == 1)
         def _():
             if steps > 2:
                 add_bias(2)
+            for d in (1, 2, 3, 0):
+                for side in (0, 1):
+                    near_wait(side, d)
+                rows = rows_of(d)
+                both = near_in[0, :, rows].astype(jnp.float32) + near_in[1, :, rows].astype(jnp.float32)
+                both = parts[1, :, rows] + both
+                if d == 0:
+                    parts[1, :, rows] = both
+                else:
+                    col_out[:, rows] = both.astype(jnp.bfloat16)
+                    col_copy(d).start()
 
         @pl.when(step == 0)
         def _():
@@ -272,13 +315,6 @@
     reply_store = pltpu.make_async_copy(rg_v, rg_hbm.at[0, 0], out_sem.at[0])
     reply_store.start()
     bias_out[...] = jnp.sum(bias_y[steps], axis=0, keepdims=True)
-
-    for side in (0, 1):
-        arrived(near_in.at[side], near_send.at[side], near_recv.at[side], at_x(1 - 2 * side))
-    parts[1] = parts[1] + (near_in[0].astype(jnp.float32) + near_in[1].astype(jnp.float32))
-    col_out[...] = parts[1].astype(jnp.bfloat16)
-    for d in range(1, ZS):
-        col_copy(d).start()
 
     for j in range(HEADS):
         cols = slice(j * HD, (j + 1) * HD)
@@ -297,9 +333,11 @@
         pg_v[side] = total.astype(jnp.bfloat16)
     prompt_store = pltpu.make_async_copy(pg_v, pg_hbm.at[0], out_sem.at[2])
     prompt_store.start()
-    started = [z_copy(d) for d in range(1, ZS)] + [col_copy(d) for d in range(1, ZS)]
-    started += [x_copy(side, d) for side in (0, 1) for d in range(ZS)]
-    started += [f(side) for f in (relay_copy, far_copy, near_copy) for side in (0, 1)]
+    started = [z_copy(kind, d) for kind in (0, 1) for d in range(1, ZS)]
+    started += [x_copy(kind, side, d) for kind in (0, 1) for side in (0, 1) for d in range(ZS)]
+    started += [relay_copy(kind, side) for kind in (0, 1) for side in (0, 1)]
+    started += [far_copy(side) for side in (0, 1)] + [col_copy(d) for d in range(1, ZS)]
+    started += [near_copy(side, d) for side in (0, 1) for d in range(ZS)]
     started += [bz_copy(d) for d in range(1, ZS)] + [bx_copy(d) for d in range(1, XS)]
     started += [by_copy(i) for i in range(steps)]
     for copy in started:
@@ -310,16 +348,9 @@
 
 
 def hand_over(*refs):
-    sem = refs[-1]
-    half = (len(refs) - 1) // 2
-    copies = [
-        pltpu.make_async_copy(src, dst, sem.at[i])
-        for i, (src, dst) in enumerate(zip(refs[:half], refs[half : 2 * half]))
-    ]
-    for copy in copies:
-        copy.start()
-    for copy in copies:
-        copy.wait()
+    half = len(refs) // 2
+    for src, dst in zip(refs[:half], refs[half:]):
+        dst[...] = src[...]
 
 
 def on_device(groups, queries, reply_kv, prompt_kv, saved_out, grad_out, prompt_len, reply_len):
@@ -347,7 +378,6 @@
             vmem((XS + 1, 2, BLOCK, HD), half),
             vmem((BLOCK, ROWS), full),
             vmem((5, BLOCK, lanes), full),
-            vmem((5, BLOCK, lanes), full),
             vmem((5 * BLOCK, lanes), half),
             vmem((HD, 5 * BLOCK), half),
             vmem((5, HEADS, ROWS), full),
@@ -369,8 +399,8 @@
             vmem((2, ROWS, HD), half),
             vmem((2, SLICE, HD), half),
             dma((5,)), dma((3,)),
-            dma((ZS,)), dma((ZS,)), dma((2, ZS)), dma((2, ZS)), dma((2,)), dma((2,)),
-            dma((2,)), dma((2,)), dma((2,)), dma((2,)), dma((ZS,)), dma((ZS,)),
+            dma((2, ZS)), dma((2, ZS)), dma((2, 2, ZS)), dma((2, 2, ZS)), dma((2, 2)), dma((2, 2)),
+            dma((2,)), dma((2,)), dma((2, ZS)), dma((2, ZS)), dma((ZS,)), dma((ZS,)),
             dma((ZS,)), dma((ZS,)), dma((XS,)), dma((XS,)),
             dma((max(steps, 1),)), dma((max(steps, 1),)),
         ],
@@ -386,9 +416,8 @@
     query_grad, reply_grad, prompt_grad, bias = pl.pallas_call(
         hand_over,
         out_shape=tuple(jax.ShapeDtypeStruct(r.shape, r.dtype) for r in results),
-        in_specs=[anywhere] * 4,
-        out_specs=(anywhere,) * 4,
-        scratch_shapes=[dma((4,))],
+        in_specs=[pl.BlockSpec(memory_space=vmem)] * 4,
+        out_specs=(pl.BlockSpec(memory_space=vmem),) * 4,
         compiler_params=pltpu.CompilerParams(vmem_limit_bytes=60 * 2**20),
     )(*results)
     return query_grad, reply_grad, prompt_grad, bias.reshape(HD)

time: 65.6 us -> 45.2 us (0.69)
  Pallas kernels: 63.5 us -> 43.1 us
    pallas_call x1, Pallas kernels: 22 us -> 1.97 us  [on_device(): pl.pallas_call(hand_over, out_shape=tuple((jax.ShapeDtypeStruct(r.shape,...]
where the time goes in v3:
time: 45.2 us; the launch traced here: 45 us
  Pallas kernels  43.1 us (95%)
  between operations  1.93 us (4%)
    pallas_call x1, Pallas kernels, on_device(): pl.pallas_call(functools.partial(kernel, groups), out_shape=(jax.ShapeDty...  41.1 us
    pallas_call x1, Pallas kernels, on_device(): pl.pallas_call(hand_over, out_shape=tuple((jax.ShapeDtypeStruct(r.shape,...  1.97 us

profile of v3, /device:TPU:8, one launch (start us, length us, event | category | flops | bytes accessed | tf_op | source)
XLA Modules:
  0.0 45.0 jit_solution(9929004242721301102)
XLA Ops:
  1.9 41.1 %shard_map.102 = (bf16[1,1,256,1024]{3,2,1,0:T(8,128)(2,1)}, bf16[1,1,2,256,128]{4,3,2,1,0:T(8,128)(2,1)}, bf16[1,2,64,128]{3,2,1,0:T(8,128)(2,1)}, f32[1,128]{1,0:T(1,128)}) custom-call(s32[1,1]{1,0:T(1,128)} %bitcast.2.plen_ref, s32[1,1]{1,0:T(1,128)S(6)} %copy.12.rlen_ref, bf16[1,1,256,1024]{3,2,1,0:T(8,128)(2,1)} %q_hbm.1, ...), custom_call_target="tpu_custom_call" | custom-call | flops 3355443200 | bytes 5242880 | tf_op jit(solution)/shard_map/pallas_call | solution.py:364
  43.1 2.0 %shard_map.103 = (bf16[1,1,256,1024]{3,2,1,0:T(8,128)(2,1)}, bf16[1,1,2,256,128]{4,3,2,1,0:T(8,128)(2,1)}, bf16[1,2,64,128]{3,2,1,0:T(8,128)(2,1)}, f32[1,128]{1,0:T(1,128)}) custom-call(bf16[1,1,256,1024]{3,2,1,0:T(8,128)(2,1)} %get-tuple-element.12.refs_0_, bf16[1,1,2,256,128]{4,3,2,1,0:T(8,128)(2,1)} %get-tuple-element.13.refs_1_, ...), custom_call_target="tpu_custom_call" | custom-call | tf_op jit(solution)/shard_map/pallas_call | solution.py:416

commit v4 on v3

--- a/solution.py
+++ b/solution.py
@@ -28,7 +28,7 @@
     groups,
     plen_ref, rlen_ref, q_hbm, rkv_hbm, pkv_hbm, o_hbm, do_hbm,
     qg_hbm, rg_hbm, pg_hbm, bias_out,
-    q_v, do_v, o_v, kv, mask, probs, dscores, keys_t,
+    q_v, do_v, o_v, q_st, do_st, q_t, do_t, kv, mask, probs, prob_b, score_b, dscores, keys_t,
     tops, totals, factors, rowdots, parts,
     far_out, far_in, near_out, near_in, col_out, col_in,
     bias_z, bias_x, bias_y, bias_in, qg_v, rg_v, pg_v,
@@ -155,7 +155,8 @@
     for j in range(HEADS):
         cols = slice(j * HD, (j + 1) * HD)
         grad = jnp.where(live, do_v[:, cols].astype(jnp.float32), 0.0)
-        do_v[:, cols] = grad.astype(jnp.bfloat16)
+        do_st[j * ROWS : (j + 1) * ROWS, :] = grad.astype(jnp.bfloat16)
+        do_t[j] = grad.T.astype(jnp.bfloat16)
         bias = bias + jnp.sum(grad.reshape(ROWS // 8, 8, HD), axis=0)
         product = grad * o_v[:, cols].astype(jnp.float32)
         high = product.astype(jnp.bfloat16)
@@ -174,6 +175,10 @@
     forward(0)
     for i in (3, 4):
         loads[i].wait()
+    for j in range(HEADS):
+        query = q_v[:, j * HD : (j + 1) * HD]
+        q_st[j * ROWS : (j + 1) * ROWS, :] = query
+        q_t[j] = query.astype(jnp.float32).T.astype(jnp.bfloat16)
     prompt_limit = plen_ref[...]
     key_row = lax.broadcasted_iota(jnp.int32, (BLOCK, ROWS), 0)
     query_row = lax.broadcasted_iota(jnp.int32, (BLOCK, ROWS), 1)
@@ -233,9 +238,8 @@
         columns = pl.ds(pl.multiple_of(step * BLOCK, BLOCK), BLOCK)
         keys_t[:, columns] = key.astype(jnp.float32).T.astype(jnp.bfloat16)
         for j in range(HEADS):
-            cols = slice(j * HD, (j + 1) * HD)
             lanes = slice(j * ROWS, (j + 1) * ROWS)
-            logits = dot(key, q_v[:, cols], NT) * to_log2 + mask[...]
+            logits = dot(key, q_t[j]) * to_log2 + mask[...]
             top = jnp.max(logits, axis=0, keepdims=True)
             power = jnp.exp2(logits - top)
             probs[step, :, lanes] = power
@@ -258,20 +262,17 @@
     def second_pass(turn, carry):
         step = 4 - turn
         value = kv[source(step)[2], 1]
-        key_part = jnp.zeros((BLOCK, HD), jnp.float32)
-        value_part = jnp.zeros((BLOCK, HD), jnp.float32)
         rows = pl.ds(pl.multiple_of(step * BLOCK, BLOCK), BLOCK)
         for j in range(HEADS):
-            cols = slice(j * HD, (j + 1) * HD)
             lanes = slice(j * ROWS, (j + 1) * ROWS)
             prob = probs[step, :, lanes] * factors[step, j : j + 1, :]
-            dprob = dot(value, do_v[:, cols], NT) - rowdots[j, 0:1, :]
+            dprob = dot(value, do_t[j]) - rowdots[j, 0:1, :]
             score = (prob * dprob).astype(jnp.bfloat16)
             dscores[rows, lanes] = score
-            value_part = value_part + dot(prob.astype(jnp.bfloat16), do_v[:, cols])
-            key_part = key_part + dot(score, q_v[:, cols])
-        parts[step, 0] = key_part * scale
-        parts[step, 1] = value_part
+            prob_b[:, lanes] = prob.astype(jnp.bfloat16)
+            score_b[:, lanes] = score
+        parts[step, 0] = dot(score_b[...], q_st[...]) * scale
+        parts[step, 1] = dot(prob_b[...], do_st[...])
 
         @pl.when(step == 4)
         def _():
@@ -375,9 +376,15 @@
             vmem((ROWS, wide), half),
             vmem((ROWS, wide), half),
             vmem((ROWS, wide), half),
+            vmem((lanes, HD), half),
+            vmem((lanes, HD), half),
+            vmem((HEADS, HD, ROWS), half),
+            vmem((HEADS, HD, ROWS), half),
             vmem((XS + 1, 2, BLOCK, HD), half),
             vmem((BLOCK, ROWS), full),
             vmem((5, BLOCK, lanes), full),
+            vmem((BLOCK, lanes), half),
+            vmem((BLOCK, lanes), half),
             vmem((5 * BLOCK, lanes), half),
             vmem((HD, 5 * BLOCK), half),
             vmem((5, HEADS, ROWS), full),

time: 45.2 us -> 45.3 us (level)
  no operation moved by 1% of the time
where the time goes in v4:
time: 45.3 us; the launch traced here: 45.1 us
  Pallas kernels  43.2 us (95%)
  between operations  1.93 us (4%)
    pallas_call x1, Pallas kernels, on_device(): pl.pallas_call(functools.partial(kernel, groups), out_shape=(jax.ShapeDty...  41.2 us
    pallas_call x1, Pallas kernels, on_device(): pl.pallas_call(hand_over, out_shape=tuple((jax.ShapeDtypeStruct(r.shape,...  1.97 us

profile of v4, /device:TPU:8, one launch (start us, length us, event | category | flops | bytes accessed | tf_op | source)
XLA Modules:
  0.0 45.1 jit_solution(2699160907448176145)
XLA Ops:
  1.9 41.2 %shard_map.102 = (bf16[1,1,256,1024]{3,2,1,0:T(8,128)(2,1)}, bf16[1,1,2,256,128]{4,3,2,1,0:T(8,128)(2,1)}, bf16[1,2,64,128]{3,2,1,0:T(8,128)(2,1)}, f32[1,128]{1,0:T(1,128)}) custom-call(s32[1,1]{1,0:T(1,128)} %bitcast.2.plen_ref, s32[1,1]{1,0:T(1,128)S(6)} %copy.12.rlen_ref, bf16[1,1,256,1024]{3,2,1,0:T(8,128)(2,1)} %q_hbm.1, ...), custom_call_target="tpu_custom_call" | custom-call | flops 3355443200 | bytes 5242880 | tf_op jit(solution)/shard_map/pallas_call | solution.py:365
  43.1 2.0 %shard_map.103 = (bf16[1,1,256,1024]{3,2,1,0:T(8,128)(2,1)}, bf16[1,1,2,256,128]{4,3,2,1,0:T(8,128)(2,1)}, bf16[1,2,64,128]{3,2,1,0:T(8,128)(2,1)}, f32[1,128]{1,0:T(1,128)}) custom-call(bf16[1,1,256,1024]{3,2,1,0:T(8,128)(2,1)} %get-tuple-element.12.refs_0_, bf16[1,1,2,256,128]{4,3,2,1,0:T(8,128)(2,1)} %get-tuple-element.13.refs_1_, ...), custom_call_target="tpu_custom_call" | custom-call | tf_op jit(solution)/shard_map/pallas_call | solution.py:423

commit v5 on v4

--- a/solution.py
+++ b/solution.py
@@ -31,7 +31,7 @@
     q_v, do_v, o_v, q_st, do_st, q_t, do_t, kv, mask, probs, prob_b, score_b, dscores, keys_t,
     tops, totals, factors, rowdots, parts,
     far_out, far_in, near_out, near_in, col_out, col_in,
-    bias_z, bias_x, bias_y, bias_in, qg_v, rg_v, pg_v,
+    bias_z, bias_x, bias_y, qg_v, rg_v, pg_v,
     local_sem, out_sem, z_send, z_recv, x_send, x_recv, relay_send, relay_recv,
     far_send, far_recv, near_send, near_recv, col_send, col_recv,
     bz_send, bz_recv, bx_send, bx_recv, by_send, by_recv,
@@ -42,7 +42,6 @@
     z = reply % ZS
     scale = HD ** (-0.5)
     to_log2 = scale * math.log2(math.e)
-    steps = groups.bit_length() - 1
 
     def at_z(d):
         return {"reply": x * ZS + (z + d) % ZS}
@@ -50,9 +49,8 @@
     def at_x(d):
         return {"reply": ((x + d) % XS) * ZS + z}
 
-    def across(i):
-        bit = 1 << i
-        return {"grp": group + bit - 2 * bit * ((group // bit) % 2)}
+    def at_group(d):
+        return {"grp": (group + d) % groups}
 
     def remote(src, dst, send, recv, device):
         return pltpu.make_async_remote_copy(
@@ -68,7 +66,7 @@
 
     barrier = pltpu.get_barrier_semaphore()
     partners = [at_z(d) for d in range(1, ZS)] + [at_x(d) for d in range(1, XS)]
-    partners += [across(i) for i in range(steps)]
+    partners += [at_group(d) for d in range(1, groups)]
     for device in partners:
         pl.semaphore_signal(barrier, inc=1, device_id=device, device_id_type=pl.DeviceIdType.MESH)
 
@@ -135,8 +133,8 @@
     def bx_copy(d):
         return remote(bias_x.at[x], bias_x.at[x], bx_send.at[d], bx_recv.at[d], at_x(d))
 
-    def by_copy(i):
-        return remote(bias_y.at[i], bias_in.at[i], by_send.at[i], by_recv.at[i], across(i))
+    def by_copy(d):
+        return remote(bias_y.at[group], bias_y.at[group], by_send.at[d], by_recv.at[d], at_group(d))
 
     loads[0].wait()
     pl.semaphore_wait(barrier, len(partners))
@@ -172,7 +170,6 @@
             for side in (0, 1):
                 x_copy(kind, side, d).start()
 
-    forward(0)
     for i in (3, 4):
         loads[i].wait()
     for j in range(HEADS):
@@ -183,12 +180,6 @@
     key_row = lax.broadcasted_iota(jnp.int32, (BLOCK, ROWS), 0)
     query_row = lax.broadcasted_iota(jnp.int32, (BLOCK, ROWS), 1)
 
-    def add_bias(i):
-        arrived(bias_in.at[i], by_send.at[i], by_recv.at[i], across(i))
-        bias_y[i + 1] = bias_y[i] + bias_in[i]
-        if i + 1 < steps:
-            by_copy(i + 1).start()
-
     def source(step):
         from_reply = 1 - (step + 3) // 4
         turn = step + 3 - 4 * ((step + 3) // 4)
@@ -198,38 +189,30 @@
     def first_pass(step, carry):
         @pl.when(step == 1)
         def _():
+            forward(0)
             forward(1)
+
+        @pl.when(step == 2)
+        def _():
+            for side in (0, 1):
+                x_wait(0, side)
+                relay_copy(0, side).start()
+
+        @pl.when(step == 3)
+        def _():
+            for side in (0, 1):
+                x_wait(1, side)
+                relay_copy(1, side).start()
             for d in range(1, ZS):
                 arrived(bias_z.at[(z - d) % ZS], bz_send.at[d], bz_recv.at[d], at_z(d))
             bias_x[x] = (bias_z[0] + bias_z[1]) + (bias_z[2] + bias_z[3])
             for d in range(1, XS):
                 bx_copy(d).start()
 
-        @pl.when(step == 2)
-        def _():
-            for side in (0, 1):
-                x_wait(0, side)
-                relay_copy(0, side).start()
-            for d in range(1, XS):
-                arrived(bias_x.at[(x - d) % XS], bx_send.at[d], bx_recv.at[d], at_x(d))
-            bias_y[0] = (bias_x[0] + bias_x[1]) + (bias_x[2] + bias_x[3])
-            if steps > 0:
-                by_copy(0).start()
-
-        @pl.when(step == 3)
-        def _():
-            for side in (0, 1):
-                x_wait(1, side)
-                relay_copy(1, side).start()
-            if steps > 0:
-                add_bias(0)
-
         @pl.when(step == 4)
         def _():
             for side in (0, 1):
                 relay_wait(0, side)
-            if steps > 1:
-                add_bias(1)
 
         from_reply, owner, block = source(step)
         last = from_reply * query_row + (1 - from_reply) * (prompt_limit - 1 - owner * BLOCK)
@@ -290,11 +273,15 @@
                 near_out[side, other] = parts[slot, other].astype(jnp.bfloat16)
                 for d in (1, 2, 3, 0):
                     near_copy(side, d).start()
+                if slot == 2:
+                    for d in range(1, XS):
+                        arrived(bias_x.at[(x - d) % XS], bx_send.at[d], bx_recv.at[d], at_x(d))
+                    bias_y[group] = (bias_x[0] + bias_x[1]) + (bias_x[2] + bias_x[3])
+                    for d in range(1, groups):
+                        by_copy(d).start()
 
         @pl.when(step == 1)
         def _():
-            if steps > 2:
-                add_bias(2)
             for d in (1, 2, 3, 0):
                 for side in (0, 1):
                     near_wait(side, d)
@@ -315,8 +302,6 @@
     lax.fori_loop(0, 5, second_pass, 0)
     reply_store = pltpu.make_async_copy(rg_v, rg_hbm.at[0, 0], out_sem.at[0])
     reply_store.start()
-    bias_out[...] = jnp.sum(bias_y[steps], axis=0, keepdims=True)
-
     for j in range(HEADS):
         cols = slice(j * HD, (j + 1) * HD)
         lanes = slice(j * ROWS, (j + 1) * ROWS)
@@ -334,13 +319,16 @@
         pg_v[side] = total.astype(jnp.bfloat16)
     prompt_store = pltpu.make_async_copy(pg_v, pg_hbm.at[0], out_sem.at[2])
     prompt_store.start()
+    for d in range(1, groups):
+        arrived(bias_y.at[(group - d) % groups], by_send.at[d], by_recv.at[d], at_group(d))
+    bias_out[...] = jnp.sum(jnp.sum(bias_y[...], axis=0), axis=0, keepdims=True)
     started = [z_copy(kind, d) for kind in (0, 1) for d in range(1, ZS)]
     started += [x_copy(kind, side, d) for kind in (0, 1) for side in (0, 1) for d in range(ZS)]
     started += [relay_copy(kind, side) for kind in (0, 1) for side in (0, 1)]
     started += [far_copy(side) for side in (0, 1)] + [col_copy(d) for d in range(1, ZS)]
     started += [near_copy(side, d) for side in (0, 1) for d in range(ZS)]
     started += [bz_copy(d) for d in range(1, ZS)] + [bx_copy(d) for d in range(1, XS)]
-    started += [by_copy(i) for i in range(steps)]
+    started += [by_copy(d) for d in range(1, groups)]
     for copy in started:
         copy.wait_send()
     reply_store.wait()
@@ -359,7 +347,6 @@
     vmem = pltpu.VMEM
     dma = pltpu.SemaphoreType.DMA
     anywhere = pl.BlockSpec(memory_space=pl.ANY)
-    steps = groups.bit_length() - 1
     wide = HEADS * HD
     lanes = HEADS * ROWS
     results = pl.pallas_call(
@@ -400,8 +387,7 @@
             vmem((ZS, 2, SLICE, HD), half),
             vmem((ZS, 8, HD), full),
             vmem((XS, 8, HD), full),
-            vmem((steps + 1, 8, HD), full),
-            vmem((max(steps, 1), 8, HD), full),
+            vmem((groups, 8, HD), full),
             vmem((ROWS, wide), half),
             vmem((2, ROWS, HD), half),
             vmem((2, SLICE, HD), half),
@@ -409,7 +395,7 @@
             dma((2, ZS)), dma((2, ZS)), dma((2, 2, ZS)), dma((2, 2, ZS)), dma((2, 2)), dma((2, 2)),
             dma((2,)), dma((2,)), dma((2, ZS)), dma((2, ZS)), dma((ZS,)), dma((ZS,)),
             dma((ZS,)), dma((ZS,)), dma((XS,)), dma((XS,)),
-            dma((max(steps, 1),)), dma((max(steps, 1),)),
+            dma((groups,)), dma((groups,)),
         ],
         compiler_params=pltpu.CompilerParams(
             collective_id=0, has_side_effects=True, vmem_limit_bytes=56 * 2**20

time: 45.3 us -> 41.9 us (0.925)
  Pallas kernels: 43.2 us -> 39.8 us
    pallas_call x1, Pallas kernels: 41.2 us -> 37.8 us  [on_device(): pl.pallas_call(functools.partial(kernel, groups), out_shape=(jax.ShapeDty...]
where the time goes in v5:
time: 41.9 us; the launch traced here: 41.7 us
  Pallas kernels  39.8 us (95%)
  between operations  1.93 us (5%)
    pallas_call x1, Pallas kernels, on_device(): pl.pallas_call(functools.partial(kernel, groups), out_shape=(jax.ShapeDty...  37.8 us
    pallas_call x1, Pallas kernels, on_device(): pl.pallas_call(hand_over, out_shape=tuple((jax.ShapeDtypeStruct(r.shape,...  1.97 us

profile of v5, /device:TPU:8, one launch (start us, length us, event | category | flops | bytes accessed | tf_op | source)
XLA Modules:
  0.0 41.7 jit_solution(4594323925962236076)
XLA Ops:
  1.9 37.8 %shard_map.102 = (bf16[1,1,256,1024]{3,2,1,0:T(8,128)(2,1)}, bf16[1,1,2,256,128]{4,3,2,1,0:T(8,128)(2,1)}, bf16[1,2,64,128]{3,2,1,0:T(8,128)(2,1)}, f32[1,128]{1,0:T(1,128)}) custom-call(s32[1,1]{1,0:T(1,128)} %bitcast.2.plen_ref, s32[1,1]{1,0:T(1,128)S(6)} %copy.12.rlen_ref, bf16[1,1,256,1024]{3,2,1,0:T(8,128)(2,1)} %q_hbm.1, ...), custom_call_target="tpu_custom_call" | custom-call | flops 3355443200 | bytes 5242880 | tf_op jit(solution)/shard_map/pallas_call | solution.py:352
  39.7 2.0 %shard_map.103 = (bf16[1,1,256,1024]{3,2,1,0:T(8,128)(2,1)}, bf16[1,1,2,256,128]{4,3,2,1,0:T(8,128)(2,1)}, bf16[1,2,64,128]{3,2,1,0:T(8,128)(2,1)}, f32[1,128]{1,0:T(1,128)}) custom-call(bf16[1,1,256,1024]{3,2,1,0:T(8,128)(2,1)} %get-tuple-element.12.refs_0_, bf16[1,1,2,256,128]{4,3,2,1,0:T(8,128)(2,1)} %get-tuple-element.13.refs_1_, ...), custom_call_target="tpu_custom_call" | custom-call | tf_op jit(solution)/shard_map/pallas_call | solution.py:409

commit v6 on v5

--- a/solution.py
+++ b/solution.py
@@ -28,12 +28,12 @@
     groups,
     plen_ref, rlen_ref, q_hbm, rkv_hbm, pkv_hbm, o_hbm, do_hbm,
     qg_hbm, rg_hbm, pg_hbm, bias_out,
-    q_v, do_v, o_v, q_st, do_st, q_t, do_t, kv, mask, probs, prob_b, score_b, dscores, keys_t,
+    q_v, do_v, o_v, q_st, do_st, q_t, do_t, kv, mask, probs, dps, prob_b, score_b, dscores, keys_t,
     tops, totals, factors, rowdots, parts,
-    far_out, far_in, near_out, near_in, col_out, col_in,
+    near_out, near_in, col_out, col_in,
     bias_z, bias_x, bias_y, qg_v, rg_v, pg_v,
     local_sem, out_sem, z_send, z_recv, x_send, x_recv, relay_send, relay_recv,
-    far_send, far_recv, near_send, near_recv, col_send, col_recv,
+    near_send, near_recv, col_send, col_recv,
     bz_send, bz_recv, bx_send, bx_recv, by_send, by_recv,
 ):
     group = lax.axis_index("grp")
@@ -87,41 +87,36 @@
     def z_wait(kind, d):
         arrived(kv.at[x, kind, rows_of(-d)], z_send.at[kind, d], z_recv.at[kind, d], at_z(d))
 
-    def x_copy(kind, side, d):
+    def x_copy(kind, way, d):
         place = kv.at[x, kind, rows_of(-d)]
-        return remote(place, place, x_send.at[kind, side, d], x_recv.at[kind, side, d],
-                      at_x(1 - 2 * side))
-
-    def x_wait(kind, side):
-        way = 1 - 2 * side
+        return remote(place, place, x_send.at[kind, way, d], x_recv.at[kind, way, d], at_x(way))
+
+    def x_wait(kind, way):
         for d in range(ZS):
-            arrived(kv.at[(x - way) % XS, kind, rows_of(-d)], x_send.at[kind, side, d],
-                    x_recv.at[kind, side, d], at_x(way))
+            arrived(kv.at[(x - way) % XS, kind, rows_of(-d)], x_send.at[kind, way, d],
+                    x_recv.at[kind, way, d], at_x(way))
+
+    x_ways = ((1, 3, 2), (1, 3))
 
     def half_of(side):
         return pl.ds(side * (BLOCK // 2), BLOCK // 2)
 
-    def relay_copy(kind, side):
+    def relay_copy(side):
         way = 1 - 2 * side
-        place = kv.at[(x - way) % XS, kind, half_of(side)]
-        return remote(place, place, relay_send.at[kind, side], relay_recv.at[kind, side],
-                      at_x(way))
-
-    def relay_wait(kind, side):
-        arrived(kv.at[(x + 2) % XS, kind, half_of(side)], relay_send.at[kind, side],
-                relay_recv.at[kind, side], at_x(1 - 2 * side))
-
-    def far_copy(side):
-        return remote(far_out.at[side], far_in.at[side], far_send.at[side], far_recv.at[side],
-                      at_x(1 - 2 * side))
-
-    def near_copy(side, d):
-        return remote(near_out.at[side, :, rows_of(d)], near_in.at[side, :, rows_of(d)],
-                      near_send.at[side, d], near_recv.at[side, d], at_x(1 - 2 * side))
-
-    def near_wait(side, d):
-        arrived(near_in.at[side, :, rows_of(d)], near_send.at[side, d], near_recv.at[side, d],
-                at_x(1 - 2 * side))
+        place = kv.at[(x - way) % XS, 1, half_of(side)]
+        return remote(place, place, relay_send.at[side], relay_recv.at[side], at_x(way))
+
+    def relay_wait(side):
+        arrived(kv.at[(x + 2) % XS, 1, half_of(side)], relay_send.at[side],
+                relay_recv.at[side], at_x(1 - 2 * side))
+
+    def near_copy(way, d):
+        return remote(near_out.at[way, :, rows_of(d)], near_in.at[way, :, rows_of(d)],
+                      near_send.at[way, d], near_recv.at[way, d], at_x(way))
+
+    def near_wait(way, d):
+        arrived(near_in.at[way, :, rows_of(d)], near_send.at[way, d], near_recv.at[way, d],
+                at_x(way))
 
     def col_copy(d):
         return remote(col_out.at[:, rows_of(d)], col_in.at[d], col_send.at[d], col_recv.at[d],
@@ -141,8 +136,8 @@
     for kind in (0, 1):
         for d in range(1, ZS):
             z_copy(kind, d).start()
-        for side in (0, 1):
-            x_copy(kind, side, 0).start()
+        for way in x_ways[kind]:
+            x_copy(kind, way, 0).start()
 
     for i in (1, 2):
         loads[i].wait()
@@ -167,8 +162,8 @@
     def forward(kind):
         for d in range(1, ZS):
             z_wait(kind, d)
-            for side in (0, 1):
-                x_copy(kind, side, d).start()
+            for way in x_ways[kind]:
+                x_copy(kind, way, d).start()
 
     for i in (3, 4):
         loads[i].wait()
@@ -186,33 +181,37 @@
         owner = (x + turn + turn // 2 - 2 * (turn // 3)) % XS
         return from_reply, owner, from_reply * XS + (1 - from_reply) * owner
 
+    def value_grads(step):
+        value = kv[source(step)[2], 1]
+        for j in range(HEADS):
+            lanes = slice(j * ROWS, (j + 1) * ROWS)
+            dps[step, :, lanes] = dot(value, do_t[j]) - rowdots[j, 0:1, :]
+
     def first_pass(step, carry):
         @pl.when(step == 1)
         def _():
             forward(0)
             forward(1)
 
-        @pl.when(step == 2)
-        def _():
-            for side in (0, 1):
-                x_wait(0, side)
-                relay_copy(0, side).start()
-
         @pl.when(step == 3)
         def _():
             for side in (0, 1):
-                x_wait(1, side)
-                relay_copy(1, side).start()
+                x_wait(1, 1 + 2 * side)
+                relay_copy(side).start()
             for d in range(1, ZS):
                 arrived(bias_z.at[(z - d) % ZS], bz_send.at[d], bz_recv.at[d], at_z(d))
             bias_x[x] = (bias_z[0] + bias_z[1]) + (bias_z[2] + bias_z[3])
             for d in range(1, XS):
                 bx_copy(d).start()
 
-        @pl.when(step == 4)
+        @pl.when(step > 0)
         def _():
-            for side in (0, 1):
-                relay_wait(0, side)
+            value_grads(step - 1)
+
+        for slot, way in ((2, 3), (3, 1), (4, 2)):
+            @pl.when(step == slot)
+            def _():
+                x_wait(0, way)
 
         from_reply, owner, block = source(step)
         last = from_reply * query_row + (1 - from_reply) * (prompt_limit - 1 - owner * BLOCK)
@@ -240,39 +239,28 @@
         factors[slot] = jnp.exp2(tops[slot] - top) / total
 
     for side in (0, 1):
-        relay_wait(1, side)
+        relay_wait(side)
+    value_grads(4)
 
     def second_pass(turn, carry):
         step = 4 - turn
-        value = kv[source(step)[2], 1]
         rows = pl.ds(pl.multiple_of(step * BLOCK, BLOCK), BLOCK)
         for j in range(HEADS):
             lanes = slice(j * ROWS, (j + 1) * ROWS)
             prob = probs[step, :, lanes] * factors[step, j : j + 1, :]
-            dprob = dot(value, do_t[j]) - rowdots[j, 0:1, :]
-            score = (prob * dprob).astype(jnp.bfloat16)
+            score = (prob * dps[step, :, lanes]).astype(jnp.bfloat16)
             dscores[rows, lanes] = score
             prob_b[:, lanes] = prob.astype(jnp.bfloat16)
             score_b[:, lanes] = score
         parts[step, 0] = dot(score_b[...], q_st[...]) * scale
         parts[step, 1] = dot(prob_b[...], do_st[...])
 
-        @pl.when(step == 4)
-        def _():
-            far_out[...] = parts[4].astype(jnp.bfloat16)
-            for side in (0, 1):
-                far_copy(side).start()
-
-        for side, slot in ((0, 2), (1, 3)):
+        for slot, way in ((4, 2), (3, 3), (2, 1)):
             @pl.when(step == slot)
             def _():
-                arrived(far_in.at[side], far_send.at[side], far_recv.at[side], at_x(1 - 2 * side))
-                other = 1 - side
-                both = parts[slot, side] + far_in[side].astype(jnp.float32)
-                near_out[side, side] = both.astype(jnp.bfloat16)
-                near_out[side, other] = parts[slot, other].astype(jnp.bfloat16)
+                near_out[way] = parts[slot].astype(jnp.bfloat16)
                 for d in (1, 2, 3, 0):
-                    near_copy(side, d).start()
+                    near_copy(way, d).start()
                 if slot == 2:
                     for d in range(1, XS):
                         arrived(bias_x.at[(x - d) % XS], bx_send.at[d], bx_recv.at[d], at_x(d))
@@ -283,15 +271,15 @@
         @pl.when(step == 1)
         def _():
             for d in (1, 2, 3, 0):
-                for side in (0, 1):
-                    near_wait(side, d)
                 rows = rows_of(d)
-                both = near_in[0, :, rows].astype(jnp.float32) + near_in[1, :, rows].astype(jnp.float32)
-                both = parts[1, :, rows] + both
+                total = parts[1, :, rows]
+                for way in (2, 3, 1):
+                    near_wait(way, d)
+                    total = total + near_in[way, :, rows].astype(jnp.float32)
                 if d == 0:
-                    parts[1, :, rows] = both
+                    parts[1, :, rows] = total
                 else:
-                    col_out[:, rows] = both.astype(jnp.bfloat16)
+                    col_out[:, rows] = total.astype(jnp.bfloat16)
                     col_copy(d).start()
 
         @pl.when(step == 0)
@@ -323,10 +311,9 @@
         arrived(bias_y.at[(group - d) % groups], by_send.at[d], by_recv.at[d], at_group(d))
     bias_out[...] = jnp.sum(jnp.sum(bias_y[...], axis=0), axis=0, keepdims=True)
     started = [z_copy(kind, d) for kind in (0, 1) for d in range(1, ZS)]
-    started += [x_copy(kind, side, d) for kind in (0, 1) for side in (0, 1) for d in range(ZS)]
-    started += [relay_copy(kind, side) for kind in (0, 1) for side in (0, 1)]
-    started += [far_copy(side) for side in (0, 1)] + [col_copy(d) for d in range(1, ZS)]
-    started += [near_copy(side, d) for side in (0, 1) for d in range(ZS)]
+    started += [x_copy(kind, way, d) for kind in (0, 1) for way in x_ways[kind] for d in range(ZS)]
+    started += [relay_copy(side) for side in (0, 1)] + [col_copy(d) for d in range(1, ZS)]
+    started += [near_copy(way, d) for way in range(1, XS) for d in range(ZS)]
     started += [bz_copy(d) for d in range(1, ZS)] + [bx_copy(d) for d in range(1, XS)]
     started += [by_copy(d) for d in range(1, groups)]
     for copy in started:
@@ -336,10 +323,26 @@
     prompt_store.wait()
 
 
-def hand_over(*refs):
-    half = len(refs) // 2
-    for src, dst in zip(refs[:half], refs[half:]):
-        dst[...] = src[...]
+def hand_over(
+    query_in, reply_in, prompt_in, bias_in, query_out, reply_out, prompt_out, bias_out,
+    query_v, reply_v, prompt_v, bias_v, in_sem, out_sem,
+):
+    piece = ROWS // 4
+    moves = [
+        (query_in.at[0, 0, rows], query_v.at[rows], query_out.at[0, 0, rows])
+        for rows in (pl.ds(i * piece, piece) for i in range(4))
+    ]
+    moves += [(reply_in, reply_v, reply_out), (prompt_in, prompt_v, prompt_out)]
+    moves += [(bias_in, bias_v, bias_out)]
+    enter = [pltpu.make_async_copy(m[0], m[1], in_sem.at[i]) for i, m in enumerate(moves)]
+    leave = [pltpu.make_async_copy(m[1], m[2], out_sem.at[i]) for i, m in enumerate(moves)]
+    for copy in enter:
+        copy.start()
+    for before, after in zip(enter, leave):
+        before.wait()
+        after.start()
+    for copy in leave:
+        copy.wait()
 
 
 def on_device(groups, queries, reply_kv, prompt_kv, saved_out, grad_out, prompt_len, reply_len):
@@ -370,6 +373,7 @@
             vmem((XS + 1, 2, BLOCK, HD), half),
             vmem((BLOCK, ROWS), full),
             vmem((5, BLOCK, lanes), full),
+            vmem((5, BLOCK, lanes), full),
             vmem((BLOCK, lanes), half),
             vmem((BLOCK, lanes), half),
             vmem((5 * BLOCK, lanes), half),
@@ -379,10 +383,8 @@
             vmem((5, HEADS, ROWS), full),
             vmem((HEADS, 8, ROWS), full),
             vmem((5, 2, BLOCK, HD), full),
-            vmem((2, BLOCK, HD), half),
-            vmem((2, BLOCK, HD), half),
-            vmem((2, 2, BLOCK, HD), half),
-            vmem((2, 2, BLOCK, HD), half),
+            vmem((XS, 2, BLOCK, HD), half),
+            vmem((XS, 2, BLOCK, HD), half),
             vmem((2, BLOCK, HD), half),
             vmem((ZS, 2, SLICE, HD), half),
             vmem((ZS, 8, HD), full),
@@ -392,8 +394,8 @@
             vmem((2, ROWS, HD), half),
             vmem((2, SLICE, HD), half),
             dma((5,)), dma((3,)),
-            dma((2, ZS)), dma((2, ZS)), dma((2, 2, ZS)), dma((2, 2, ZS)), dma((2, 2)), dma((2, 2)),
-            dma((2,)), dma((2,)), dma((2, ZS)), dma((2, ZS)), dma((ZS,)), dma((ZS,)),
+            dma((2, ZS)), dma((2, ZS)), dma((2, XS, ZS)), dma((2, XS, ZS)), dma((2,)), dma((2,)),
+            dma((XS, ZS)), dma((XS, ZS)), dma((ZS,)), dma((ZS,)),
             dma((ZS,)), dma((ZS,)), dma((XS,)), dma((XS,)),
             dma((groups,)), dma((groups,)),
         ],
@@ -409,8 +411,16 @@
     query_grad, reply_grad, prompt_grad, bias = pl.pallas_call(
         hand_over,
         out_shape=tuple(jax.ShapeDtypeStruct(r.shape, r.dtype) for r in results),
-        in_specs=[pl.BlockSpec(memory_space=vmem)] * 4,
-        out_specs=(pl.BlockSpec(memory_space=vmem),) * 4,
+        in_specs=[anywhere] * 4,
+        out_specs=(anywhere,) * 4,
+        scratch_shapes=[
+            vmem((ROWS, wide), half),
+            vmem(reply_kv.shape, half),
+            vmem(prompt_kv.shape, half),
+            vmem((1, HD), full),
+            dma((7,)),
+            dma((7,)),
+        ],
         compiler_params=pltpu.CompilerParams(vmem_limit_bytes=60 * 2**20),
     )(*results)
     return query_grad, reply_grad, prompt_grad, bias.reshape(HD)

time: 41.9 us -> 39 us (0.931)
  Pallas kernels: 39.8 us -> 36.9 us
    pallas_call x1, Pallas kernels: 37.8 us -> 35 us  [on_device(): pl.pallas_call(functools.partial(kernel, groups), out_shape=(jax.ShapeDty...]
where the time goes in v6:
time: 39 us; the launch traced here: 38.8 us
  Pallas kernels  36.9 us (95%)
  between operations  1.93 us (5%)
    pallas_call x1, Pallas kernels, on_device(): pl.pallas_call(functools.partial(kernel, groups), out_shape=(jax.ShapeDty...  35 us
    pallas_call x1, Pallas kernels, on_device(): pl.pallas_call(hand_over, out_shape=tuple((jax.ShapeDtypeStruct(r.shape,...  1.95 us

profile of v6, /device:TPU:8, one launch (start us, length us, event | category | flops | bytes accessed | tf_op | source)
XLA Modules:
  0.0 38.8 jit_solution(4435220622066918255)
XLA Ops:
  1.9 35.0 %shard_map.102 = (bf16[1,1,256,1024]{3,2,1,0:T(8,128)(2,1)}, bf16[1,1,2,256,128]{4,3,2,1,0:T(8,128)(2,1)}, bf16[1,2,64,128]{3,2,1,0:T(8,128)(2,1)}, f32[1,128]{1,0:T(1,128)}) custom-call(s32[1,1]{1,0:T(1,128)} %bitcast.2.plen_ref, s32[1,1]{1,0:T(1,128)S(6)} %copy.12.rlen_ref, bf16[1,1,256,1024]{3,2,1,0:T(8,128)(2,1)} %q_hbm.1, ...), custom_call_target="tpu_custom_call" | custom-call | flops 3355443200 | bytes 5242880 | tf_op jit(solution)/shard_map/pallas_call | solution.py:355
  36.9 1.9 %shard_map.103 = (bf16[1,1,256,1024]{3,2,1,0:T(8,128)(2,1)}, bf16[1,1,2,256,128]{4,3,2,1,0:T(8,128)(2,1)}, bf16[1,2,64,128]{3,2,1,0:T(8,128)(2,1)}, f32[1,128]{1,0:T(1,128)}) custom-call(bf16[1,1,256,1024]{3,2,1,0:T(8,128)(2,1)} %get-tuple-element.12.query_in, bf16[1,1,2,256,128]{4,3,2,1,0:T(8,128)(2,1)} %get-tuple-element.13.reply_in, ...), custom_call_target="tpu_custom_call" | custom-call | tf_op jit(solution)/shard_map/pallas_call | solution.py:411

commit v7 on v6

--- a/solution.py
+++ b/solution.py
@@ -30,10 +30,10 @@
     qg_hbm, rg_hbm, pg_hbm, bias_out,
     q_v, do_v, o_v, q_st, do_st, q_t, do_t, kv, mask, probs, dps, prob_b, score_b, dscores, keys_t,
     tops, totals, factors, rowdots, parts,
-    near_out, near_in, col_out, col_in,
+    near_out, near_in, col_out, col_in, last_in,
     bias_z, bias_x, bias_y, qg_v, rg_v, pg_v,
-    local_sem, out_sem, z_send, z_recv, x_send, x_recv, relay_send, relay_recv,
-    near_send, near_recv, col_send, col_recv,
+    local_sem, out_sem, key_send, key_recv, z_send, z_recv, x_send, x_recv, relay_send, relay_recv,
+    near_send, near_recv, col_send, col_recv, last_send, last_recv,
     bz_send, bz_recv, bx_send, bx_recv, by_send, by_recv,
 ):
     group = lax.axis_index("grp")
@@ -43,6 +43,9 @@
     scale = HD ** (-0.5)
     to_log2 = scale * math.log2(math.e)
 
+    def at(way, d):
+        return {"reply": ((x + way) % XS) * ZS + (z + d) % ZS}
+
     def at_z(d):
         return {"reply": x * ZS + (z + d) % ZS}
 
@@ -65,7 +68,7 @@
         return pl.ds(pl.multiple_of(((z + d) % ZS) * SLICE, SLICE), SLICE)
 
     barrier = pltpu.get_barrier_semaphore()
-    partners = [at_z(d) for d in range(1, ZS)] + [at_x(d) for d in range(1, XS)]
+    partners = [at(way, d) for way in range(XS) for d in range(ZS) if way + d > 0]
     partners += [at_group(d) for d in range(1, groups)]
     for device in partners:
         pl.semaphore_signal(barrier, inc=1, device_id=device, device_id_type=pl.DeviceIdType.MESH)
@@ -80,23 +83,28 @@
     for load in loads:
         load.start()
 
-    def z_copy(kind, d):
-        place = kv.at[x, kind, rows_of(0)]
-        return remote(place, place, z_send.at[kind, d], z_recv.at[kind, d], at_z(d))
-
-    def z_wait(kind, d):
-        arrived(kv.at[x, kind, rows_of(-d)], z_send.at[kind, d], z_recv.at[kind, d], at_z(d))
-
-    def x_copy(kind, way, d):
-        place = kv.at[x, kind, rows_of(-d)]
-        return remote(place, place, x_send.at[kind, way, d], x_recv.at[kind, way, d], at_x(way))
-
-    def x_wait(kind, way):
+    def key_copy(way, d):
+        place = kv.at[x, 0, rows_of(0)]
+        return remote(place, place, key_send.at[way, d], key_recv.at[way, d], at(way, d))
+
+    def key_wait(way):
         for d in range(ZS):
-            arrived(kv.at[(x - way) % XS, kind, rows_of(-d)], x_send.at[kind, way, d],
-                    x_recv.at[kind, way, d], at_x(way))
-
-    x_ways = ((1, 3, 2), (1, 3))
+            if way + d > 0:
+                arrived(kv.at[(x - way) % XS, 0, rows_of(-d)], key_send.at[way, d],
+                        key_recv.at[way, d], at(way, d))
+
+    def z_copy(d):
+        place = kv.at[x, 1, rows_of(0)]
+        return remote(place, place, z_send.at[d], z_recv.at[d], at_z(d))
+
+    def x_copy(way, d):
+        place = kv.at[x, 1, rows_of(-d)]
+        return remote(place, place, x_send.at[way, d], x_recv.at[way, d], at_x(way))
+
+    def x_wait(way):
+        for d in range(ZS):
+            arrived(kv.at[(x - way) % XS, 1, rows_of(-d)], x_send.at[way, d], x_recv.at[way, d],
+                    at_x(way))
 
     def half_of(side):
         return pl.ds(side * (BLOCK // 2), BLOCK // 2)
@@ -118,6 +126,13 @@
         arrived(near_in.at[way, :, rows_of(d)], near_send.at[way, d], near_recv.at[way, d],
                 at_x(way))
 
+    def last_copy(d):
+        return remote(near_out.at[1, :, rows_of(d)], last_in.at[d], last_send.at[d],
+                      last_recv.at[d], at(1, d))
+
+    def last_wait(d):
+        arrived(last_in.at[d], last_send.at[d], last_recv.at[d], at(1, d))
+
     def col_copy(d):
         return remote(col_out.at[:, rows_of(d)], col_in.at[d], col_send.at[d], col_recv.at[d],
                       at_z(d))
@@ -133,11 +148,14 @@
 
     loads[0].wait()
     pl.semaphore_wait(barrier, len(partners))
-    for kind in (0, 1):
-        for d in range(1, ZS):
-            z_copy(kind, d).start()
-        for way in x_ways[kind]:
-            x_copy(kind, way, 0).start()
+    for way in (0, 3, 1, 2):
+        for d in range(ZS):
+            if way + d > 0:
+                key_copy(way, d).start()
+    for d in range(1, ZS):
+        z_copy(d).start()
+    for way in (1, 3):
+        x_copy(way, 0).start()
 
     for i in (1, 2):
         loads[i].wait()
@@ -159,12 +177,6 @@
     for d in range(1, ZS):
         bz_copy(d).start()
 
-    def forward(kind):
-        for d in range(1, ZS):
-            z_wait(kind, d)
-            for way in x_ways[kind]:
-                x_copy(kind, way, d).start()
-
     for i in (3, 4):
         loads[i].wait()
     for j in range(HEADS):
@@ -190,13 +202,16 @@
     def first_pass(step, carry):
         @pl.when(step == 1)
         def _():
-            forward(0)
-            forward(1)
+            for d in range(1, ZS):
+                arrived(kv.at[x, 1, rows_of(-d)], z_send.at[d], z_recv.at[d], at_z(d))
+                for way in (1, 3):
+                    x_copy(way, d).start()
+            key_wait(0)
 
         @pl.when(step == 3)
         def _():
             for side in (0, 1):
-                x_wait(1, 1 + 2 * side)
+                x_wait(1 + 2 * side)
                 relay_copy(side).start()
             for d in range(1, ZS):
                 arrived(bias_z.at[(z - d) % ZS], bz_send.at[d], bz_recv.at[d], at_z(d))
@@ -211,7 +226,7 @@
         for slot, way in ((2, 3), (3, 1), (4, 2)):
             @pl.when(step == slot)
             def _():
-                x_wait(0, way)
+                key_wait(way)
 
         from_reply, owner, block = source(step)
         last = from_reply * query_row + (1 - from_reply) * (prompt_limit - 1 - owner * BLOCK)
@@ -260,7 +275,7 @@
             def _():
                 near_out[way] = parts[slot].astype(jnp.bfloat16)
                 for d in (1, 2, 3, 0):
-                    near_copy(way, d).start()
+                    (last_copy(d) if slot == 2 else near_copy(way, d)).start()
                 if slot == 2:
                     for d in range(1, XS):
                         arrived(bias_x.at[(x - d) % XS], bx_send.at[d], bx_recv.at[d], at_x(d))
@@ -273,7 +288,7 @@
             for d in (1, 2, 3, 0):
                 rows = rows_of(d)
                 total = parts[1, :, rows]
-                for way in (2, 3, 1):
+                for way in (2, 3):
                     near_wait(way, d)
                     total = total + near_in[way, :, rows].astype(jnp.float32)
                 if d == 0:
@@ -300,20 +315,26 @@
 
     for d in range(1, ZS):
         arrived(col_in.at[d], col_send.at[d], col_recv.at[d], at_z(d))
+    for d in range(ZS):
+        last_wait(d)
     for side in (0, 1):
         total = parts[1, side, rows_of(0), :]
         for d in range(1, ZS):
             total = total + col_in[d, side].astype(jnp.float32)
+        for d in range(ZS):
+            total = total + last_in[d, side].astype(jnp.float32)
         pg_v[side] = total.astype(jnp.bfloat16)
     prompt_store = pltpu.make_async_copy(pg_v, pg_hbm.at[0], out_sem.at[2])
     prompt_store.start()
     for d in range(1, groups):
         arrived(bias_y.at[(group - d) % groups], by_send.at[d], by_recv.at[d], at_group(d))
     bias_out[...] = jnp.sum(jnp.sum(bias_y[...], axis=0), axis=0, keepdims=True)
-    started = [z_copy(kind, d) for kind in (0, 1) for d in range(1, ZS)]
-    started += [x_copy(kind, way, d) for kind in (0, 1) for way in x_ways[kind] for d in range(ZS)]
+    started = [key_copy(way, d) for way in range(XS) for d in range(ZS) if way + d > 0]
+    started += [z_copy(d) for d in range(1, ZS)]
+    started += [x_copy(way, d) for way in (1, 3) for d in range(ZS)]
     started += [relay_copy(side) for side in (0, 1)] + [col_copy(d) for d in range(1, ZS)]
-    started += [near_copy(way, d) for way in range(1, XS) for d in range(ZS)]
+    started += [near_copy(way, d) for way in (2, 3) for d in range(ZS)]
+    started += [last_copy(d) for d in range(ZS)]
     started += [bz_copy(d) for d in range(1, ZS)] + [bx_copy(d) for d in range(1, XS)]
     started += [by_copy(d) for d in range(1, groups)]
     for copy in started:
@@ -387,6 +408,7 @@
             vmem((XS, 2, BLOCK, HD), half),
             vmem((2, BLOCK, HD), half),
             vmem((ZS, 2, SLICE, HD), half),
+            vmem((ZS, 2, SLICE, HD), half),
             vmem((ZS, 8, HD), full),
             vmem((XS, 8, HD), full),
             vmem((groups, 8, HD), full),
@@ -394,8 +416,9 @@
             vmem((2, ROWS, HD), half),
             vmem((2, SLICE, HD), half),
             dma((5,)), dma((3,)),
-            dma((2, ZS)), dma((2, ZS)), dma((2, XS, ZS)), dma((2, XS, ZS)), dma((2,)), dma((2,)),
-            dma((XS, ZS)), dma((XS, ZS)), dma((ZS,)), dma((ZS,)),
+            dma((XS, ZS)), dma((XS, ZS)),
+            dma((ZS,)), dma((ZS,)), dma((XS, ZS)), dma((XS, ZS)), dma((2,)), dma((2,)),
+            dma((XS, ZS)), dma((XS, ZS)), dma((ZS,)), dma((ZS,)), dma((ZS,)), dma((ZS,)),
             dma((ZS,)), dma((ZS,)), dma((XS,)), dma((XS,)),
             dma((groups,)), dma((groups,)),
         ],

time: 39 us -> 42.6 us (1.092)
  the two profiles are of different devices: /device:TPU:8 before, /device:TPU:4 now
where the time goes in v7:
time: 42.6 us; the launch traced here: 42.4 us
  Pallas kernels  40.5 us (95%)
  between operations  1.93 us (5%)
    pallas_call x1, Pallas kernels, on_device(): pl.pallas_call(functools.partial(kernel, groups), out_shape=(jax.ShapeDty...  38.5 us
    pallas_call x1, Pallas kernels, on_device(): pl.pallas_call(hand_over, out_shape=tuple((jax.ShapeDtypeStruct(r.shape,...  1.95 us

profile of v7, /device:TPU:4, one launch (start us, length us, event | category | flops | bytes accessed | tf_op | source)
XLA Modules:
  0.0 42.4 jit_solution(2458660106795966048)
XLA Ops:
  1.9 38.5 %shard_map.102 = (bf16[1,1,256,1024]{3,2,1,0:T(8,128)(2,1)}, bf16[1,1,2,256,128]{4,3,2,1,0:T(8,128)(2,1)}, bf16[1,2,64,128]{3,2,1,0:T(8,128)(2,1)}, f32[1,128]{1,0:T(1,128)}) custom-call(s32[1,1]{1,0:T(1,128)} %bitcast.2.plen_ref, s32[1,1]{1,0:T(1,128)S(6)} %copy.12.rlen_ref, bf16[1,1,256,1024]{3,2,1,0:T(8,128)(2,1)} %q_hbm.1, ...), custom_call_target="tpu_custom_call" | custom-call | flops 3355443200 | bytes 5242880 | tf_op jit(solution)/shard_map/pallas_call | solution.py:376
  40.5 1.9 %shard_map.103 = (bf16[1,1,256,1024]{3,2,1,0:T(8,128)(2,1)}, bf16[1,1,2,256,128]{4,3,2,1,0:T(8,128)(2,1)}, bf16[1,2,64,128]{3,2,1,0:T(8,128)(2,1)}, f32[1,128]{1,0:T(1,128)}) custom-call(bf16[1,1,256,1024]{3,2,1,0:T(8,128)(2,1)} %get-tuple-element.12.query_in, bf16[1,1,2,256,128]{4,3,2,1,0:T(8,128)(2,1)} %get-tuple-element.13.reply_in, ...), custom_call_target="tpu_custom_call" | custom-call | tf_op jit(solution)/shard_map/pallas_call | solution.py:434

commit v8 on v6

--- a/solution.py
+++ b/solution.py
@@ -96,19 +96,20 @@
             arrived(kv.at[(x - way) % XS, kind, rows_of(-d)], x_send.at[kind, way, d],
                     x_recv.at[kind, way, d], at_x(way))
 
-    x_ways = ((1, 3, 2), (1, 3))
+    x_ways = ((1, 3), (1, 3))
 
     def half_of(side):
         return pl.ds(side * (BLOCK // 2), BLOCK // 2)
 
-    def relay_copy(side):
+    def relay_copy(kind, side):
         way = 1 - 2 * side
-        place = kv.at[(x - way) % XS, 1, half_of(side)]
-        return remote(place, place, relay_send.at[side], relay_recv.at[side], at_x(way))
-
-    def relay_wait(side):
-        arrived(kv.at[(x + 2) % XS, 1, half_of(side)], relay_send.at[side],
-                relay_recv.at[side], at_x(1 - 2 * side))
+        place = kv.at[(x - way) % XS, kind, half_of(side)]
+        return remote(place, place, relay_send.at[kind, side], relay_recv.at[kind, side],
+                      at_x(way))
+
+    def relay_wait(kind, side):
+        arrived(kv.at[(x + 2) % XS, kind, half_of(side)], relay_send.at[kind, side],
+                relay_recv.at[kind, side], at_x(1 - 2 * side))
 
     def near_copy(way, d):
         return remote(near_out.at[way, :, rows_of(d)], near_in.at[way, :, rows_of(d)],
@@ -197,7 +198,7 @@
         def _():
             for side in (0, 1):
                 x_wait(1, 1 + 2 * side)
-                relay_copy(side).start()
+                relay_copy(1, side).start()
             for d in range(1, ZS):
                 arrived(bias_z.at[(z - d) % ZS], bz_send.at[d], bz_recv.at[d], at_z(d))
             bias_x[x] = (bias_z[0] + bias_z[1]) + (bias_z[2] + bias_z[3])
@@ -208,10 +209,16 @@
         def _():
             value_grads(step - 1)
 
-        for slot, way in ((2, 3), (3, 1), (4, 2)):
-            @pl.when(step == slot)
-            def _():
-                x_wait(0, way)
+        @pl.when(step == 2)
+        def _():
+            for side in (0, 1):
+                x_wait(0, 1 + 2 * side)
+                relay_copy(0, side).start()
+
+        @pl.when(step == 4)
+        def _():
+            for side in (0, 1):
+                relay_wait(0, side)
 
         from_reply, owner, block = source(step)
         last = from_reply * query_row + (1 - from_reply) * (prompt_limit - 1 - owner * BLOCK)
@@ -239,7 +246,7 @@
         factors[slot] = jnp.exp2(tops[slot] - top) / total
 
     for side in (0, 1):
-        relay_wait(side)
+        relay_wait(1, side)
     value_grads(4)
 
     def second_pass(turn, carry):
@@ -312,7 +319,7 @@
     bias_out[...] = jnp.sum(jnp.sum(bias_y[...], axis=0), axis=0, keepdims=True)
     started = [z_copy(kind, d) for kind in (0, 1) for d in range(1, ZS)]
     started += [x_copy(kind, way, d) for kind in (0, 1) for way in x_ways[kind] for d in range(ZS)]
-    started += [relay_copy(side) for side in (0, 1)] + [col_copy(d) for d in range(1, ZS)]
+    started += [relay_copy(kind, side) for kind in (0, 1) for side in (0, 1)] + [col_copy(d) for d in range(1, ZS)]
     started += [near_copy(way, d) for way in range(1, XS) for d in range(ZS)]
     started += [bz_copy(d) for d in range(1, ZS)] + [bx_copy(d) for d in range(1, XS)]
     started += [by_copy(d) for d in range(1, groups)]
@@ -394,7 +401,7 @@
             vmem((2, ROWS, HD), half),
             vmem((2, SLICE, HD), half),
             dma((5,)), dma((3,)),
-            dma((2, ZS)), dma((2, ZS)), dma((2, XS, ZS)), dma((2, XS, ZS)), dma((2,)), dma((2,)),
+            dma((2, ZS)), dma((2, ZS)), dma((2, XS, ZS)), dma((2, XS, ZS)), dma((2, 2)), dma((2, 2)),
             dma((XS, ZS)), dma((XS, ZS)), dma((ZS,)), dma((ZS,)),
             dma((ZS,)), dma((ZS,)), dma((XS,)), dma((XS,)),
             dma((groups,)), dma((groups,)),

time: 39 us -> 39.1 us (level)
  no operation moved by 1% of the time
where the time goes in v8:
time: 39.1 us; the launch traced here: 38.9 us
  Pallas kernels  37 us (95%)
  between operations  1.93 us (5%)
    pallas_call x1, Pallas kernels, on_device(): pl.pallas_call(functools.partial(kernel, groups), out_shape=(jax.ShapeDty...  35 us
    pallas_call x1, Pallas kernels, on_device(): pl.pallas_call(hand_over, out_shape=tuple((jax.ShapeDtypeStruct(r.shape,...  1.95 us

profile of v8, /device:TPU:8, one launch (start us, length us, event | category | flops | bytes accessed | tf_op | source)
XLA Modules:
  0.0 38.9 jit_solution(139052908294074675)
XLA Ops:
  1.9 35.0 %shard_map.102 = (bf16[1,1,256,1024]{3,2,1,0:T(8,128)(2,1)}, bf16[1,1,2,256,128]{4,3,2,1,0:T(8,128)(2,1)}, bf16[1,2,64,128]{3,2,1,0:T(8,128)(2,1)}, f32[1,128]{1,0:T(1,128)}) custom-call(s32[1,1]{1,0:T(1,128)} %bitcast.2.plen_ref, s32[1,1]{1,0:T(1,128)S(6)} %copy.12.rlen_ref, bf16[1,1,256,1024]{3,2,1,0:T(8,128)(2,1)} %q_hbm.1, ...), custom_call_target="tpu_custom_call" | custom-call | flops 3355443200 | bytes 5242880 | tf_op jit(solution)/shard_map/pallas_call | solution.py:362
  37.0 1.9 %shard_map.103 = (bf16[1,1,256,1024]{3,2,1,0:T(8,128)(2,1)}, bf16[1,1,2,256,128]{4,3,2,1,0:T(8,128)(2,1)}, bf16[1,2,64,128]{3,2,1,0:T(8,128)(2,1)}, f32[1,128]{1,0:T(1,128)}) custom-call(bf16[1,1,256,1024]{3,2,1,0:T(8,128)(2,1)} %get-tuple-element.12.query_in, bf16[1,1,2,256,128]{4,3,2,1,0:T(8,128)(2,1)} %get-tuple-element.13.reply_in, ...), custom_call_target="tpu_custom_call" | custom-call | tf_op jit(solution)/shard_map/pallas_call | solution.py:418

commit v9 on v8

--- a/solution.py
+++ b/solution.py
@@ -191,7 +191,6 @@
     def first_pass(step, carry):
         @pl.when(step == 1)
         def _():
-            forward(0)
             forward(1)
 
         @pl.when(step == 3)
@@ -236,6 +235,7 @@
             totals[step, j : j + 1, :] = jnp.sum(power, axis=0, keepdims=True)
         return carry
 
+    forward(0)
     lax.fori_loop(0, 5, first_pass, 0)
 
     top = jnp.max(tops[...], axis=0)

time: 39.1 us -> 39.4 us (level)
  no operation moved by 1% of the time
where the time goes in v9:
time: 39.4 us; the launch traced here: 39.2 us
  Pallas kernels  37.3 us (95%)
  between operations  1.93 us (5%)
    pallas_call x1, Pallas kernels, on_device(): pl.pallas_call(functools.partial(kernel, groups), out_shape=(jax.ShapeDty...  35.3 us
    pallas_call x1, Pallas kernels, on_device(): pl.pallas_call(hand_over, out_shape=tuple((jax.ShapeDtypeStruct(r.shape,...  1.95 us

profile of v9, /device:TPU:8, one launch (start us, length us, event | category | flops | bytes accessed | tf_op | source)
XLA Modules:
  0.0 39.2 jit_solution(6321579106560475031)
XLA Ops:
  1.9 35.3 %shard_map.102 = (bf16[1,1,256,1024]{3,2,1,0:T(8,128)(2,1)}, bf16[1,1,2,256,128]{4,3,2,1,0:T(8,128)(2,1)}, bf16[1,2,64,128]{3,2,1,0:T(8,128)(2,1)}, f32[1,128]{1,0:T(1,128)}) custom-call(s32[1,1]{1,0:T(1,128)} %bitcast.2.plen_ref, s32[1,1]{1,0:T(1,128)S(6)} %copy.12.rlen_ref, bf16[1,1,256,1024]{3,2,1,0:T(8,128)(2,1)} %q_hbm.1, ...), custom_call_target="tpu_custom_call" | custom-call | flops 3355443200 | bytes 5242880 | tf_op jit(solution)/shard_map/pallas_call | solution.py:362
  37.3 1.9 %shard_map.103 = (bf16[1,1,256,1024]{3,2,1,0:T(8,128)(2,1)}, bf16[1,1,2,256,128]{4,3,2,1,0:T(8,128)(2,1)}, bf16[1,2,64,128]{3,2,1,0:T(8,128)(2,1)}, f32[1,128]{1,0:T(1,128)}) custom-call(bf16[1,1,256,1024]{3,2,1,0:T(8,128)(2,1)} %get-tuple-element.12.query_in, bf16[1,1,2,256,128]{4,3,2,1,0:T(8,128)(2,1)} %get-tuple-element.13.reply_in, ...), custom_call_target="tpu_custom_call" | custom-call | tf_op jit(solution)/shard_map/pallas_call | solution.py:418
